TPU v7x, 32 devices: a whole 2x2x4 slice. The times are simulated.
32 devices in a mesh: wide: 8 (over z, y), narrow: 4 (over x, core).
Axes of the slice: x: 2, y: 2, z: 4, core: 2. Of those that a mesh axis runs over, the one named last changes fastest.
Arguments:
- prefit_resid: float32 [1310720], P(('wide', 'narrow')), may hold values from -6 to 6
- source_partials: float32 [5, 1310720], P(None, ('wide', 'narrow')), may hold values from -6 to 6
- attitude_partials: float32 [4, 1310720], P(None, ('wide', 'narrow')), may hold values from -0.25 to 0.25
- spline_position: float32 [1310720], P(('wide', 'narrow')), may hold values from 0 to 1
- calib_partials: float32 [3, 1310720], P(None, ('wide', 'narrow')), may hold values from -2 to 2
- obs_source: int32 [1310720], P(('wide', 'narrow')), may hold values from 0 to 127
- block_count: int32 [2048], P(('wide', 'narrow')), may hold values from 320 to 640, as said below
- obs_range: int32 [1310720], P(('wide', 'narrow')), may hold values from 0 to 7, as said below
- obs_knot: int32 [1310720], P(('wide', 'narrow')), may hold values from 0 to 255
- obs_unit: int32 [1310720], P(('wide', 'narrow')), may hold values from 0 to 2015
- given_inverse: float32 [8, 1024, 1024], P('wide'), may hold values from -2.5 to 2.5, as said below
- knot_decay: float32 [4, 2048], P(None, 'wide'), may hold values from 0.15 to 1
Outputs:
- source_update: float32 [5, 262144], P(None, ('wide', 'narrow'))
- attitude_update: float32 [4, 2048], P(None, 'wide')
- cal_update: float32 [3, 2016], P(None, 'narrow')
Inputs may be any that keep to these rules, and one draw needn't show every extreme that they name: `block_count`: each block's live observations are its first slots; every device has one block with all 640 slots live. `obs_range`: at most 10240 of one device's observation slots fall in one time range; for each index along narrow, some time range holds exactly 10240 slots of every device of that index. `given_inverse`: each time range's given inverse is symmetric.
All inputs are finite; a program needn't handle non-finite values.
Results may differ from a plain program's by a relative error of at most 0.0003.
Values sent between devices are 32-bit elements; how exact they have to be, the bound alone decides.
A program may use at most 64 MiB of HBM per device.

v0:
```python
import math

import jax
import jax.numpy as jnp
from jax import lax
from jax.sharding import PartitionSpec as P

SRC_BLK = 128
SLOT_BLK = 640
CAL = 2016


source_pairs = [(left_at, right_at) for left_at in range(5) for right_at in range(left_at, 5)]
calib_pairs = [(left_at, right_at) for left_at in range(3) for right_at in range(left_at, 3)]


def entering_2(value, axis, join, neutral):
    count, mine = (lax.axis_size(axis), lax.axis_index(axis))
    pieces = jax.tree.map(lambda part: lax.all_gather(part, axis), value)
    running = jax.tree.map(
        lambda part, zero: jnp.full_like(part, 0) + jnp.asarray(zero, part.dtype), value, neutral
    )

    def step(position, running):
        longer = join(running, jax.tree.map(lambda part: part[position], pieces))
        return jax.tree.map(lambda new, old: jnp.where(position < mine, new, old), longer, running)

    return lax.fori_loop(0, count - 1, step, running)


def spline(position):
    remain = 1.0 - position
    square_pos = position * position
    cube_pos = square_pos * position
    return jnp.stack(
        [
            remain * remain * remain / 6.0,
            (3.0 * cube_pos - 6.0 * square_pos + 4.0) / 6.0,
            (-3.0 * cube_pos + 3.0 * square_pos + 3.0 * position + 1.0) / 6.0,
            cube_pos / 6.0,
        ]
    )


def symmetric(values, pair_list, order_size):
    matrix = [[None] * order_size for index_lookup in range(order_size)]
    for slot_at, (left_at, right_at) in enumerate(pair_list):
        diag_add = 1.0 if left_at == right_at else 0.0
        entry_val = values[slot_at] + diag_add
        matrix[left_at][right_at] = entry_val
        matrix[right_at][left_at] = entry_val
    return matrix


def spd_solve(matrix, target):
    order_size = len(target)
    lower_tri = [[None] * order_size for index_lookup in range(order_size)]
    for column in range(order_size):
        pivot_sq = matrix[column][column]
        for before in range(column):
            pivot_sq = pivot_sq - lower_tri[column][before] * lower_tri[column][before]
        pivot_root = jnp.sqrt(pivot_sq)
        lower_tri[column][column] = pivot_root
        for row_at in range(column + 1, order_size):
            entry_val = matrix[row_at][column]
            for before in range(column):
                entry_val = entry_val - lower_tri[row_at][before] * lower_tri[column][before]
            lower_tri[row_at][column] = entry_val / pivot_root
    forward_sol = []
    for row_at in range(order_size):
        running = target[row_at]
        for before in range(row_at):
            running = running - lower_tri[row_at][before] * forward_sol[before]
        forward_sol.append(running / lower_tri[row_at][row_at])
    answer = [None] * order_size
    for row_at in reversed(range(order_size)):
        running = forward_sol[row_at]
        for before in range(row_at + 1, order_size):
            running = running - lower_tri[before][row_at] * answer[before]
        answer[row_at] = running / lower_tri[row_at][row_at]
    return answer


def chain_step(earlier, later):
    return (earlier[0] * later[0], later[0] * earlier[1] + later[1])


def pair_sum(values, first_ids, first_count, second_ids, second_count):
    row_count = values.shape[0]
    slot_count = values.shape[1]
    piece_size = math.gcd(slot_count, 2048)
    turn_count = slot_count // piece_size
    first_grid = jnp.arange(first_count, dtype=jnp.int32)
    second_grid = jnp.arange(second_count, dtype=jnp.int32)

    def accumulate(turn_at, running):
        starting_offset = turn_at * piece_size
        value_piece = lax.dynamic_slice_in_dim(values, starting_offset, piece_size, 1)
        first_piece = lax.dynamic_slice_in_dim(first_ids, starting_offset, piece_size, 0)
        second_piece = lax.dynamic_slice_in_dim(second_ids, starting_offset, piece_size, 0)
        first_hot = (first_grid[:, None] == first_piece[None, :]).astype(jnp.float32)
        left_rows = (value_piece[:, None, :] * first_hot[None, :, :]).reshape(
            row_count * first_count, piece_size
        )
        second_hot = (second_piece[:, None] == second_grid[None, :]).astype(jnp.float32)
        return running + jnp.dot(left_rows, second_hot, precision=lax.Precision.HIGHEST)

    totals = lax.fori_loop(
        0, turn_count, accumulate, jnp.zeros((row_count * first_count, second_count), jnp.float32)
    )
    return totals.reshape(row_count, first_count, second_count)


def shifted_knots(totals, knot_count):
    result = jnp.zeros((4, knot_count + 3), jnp.float32)
    for shift_at in range(4):
        result = result + jnp.pad(totals[shift_at], ((0, 0), (shift_at, 3 - shift_at)))
    return result


def on_device(
    prefit_resid,
    source_partials,
    attitude_partials,
    spline_position,
    calib_partials,
    obs_source,
    block_count,
    obs_range,
    obs_knot,
    obs_unit,
    given_inverse,
    knot_decay,
):
    ranges = lax.axis_size("wide")
    groups = lax.axis_size("narrow")
    blocks = block_count.shape[0]
    count_obs = prefit_resid.shape[0]
    knots_dev = knot_decay.shape[1]
    valid_grid = (jnp.arange(SLOT_BLK, dtype=jnp.int32)[None, :] < block_count[:, None]).astype(
        jnp.float32
    )
    valid_mask = valid_grid.reshape(count_obs)
    member = (
        obs_source.reshape(blocks, SLOT_BLK)[:, :, None]
        == jnp.arange(SRC_BLK, dtype=jnp.int32)[None, None, :]
    ).astype(jnp.float32) * valid_grid[:, :, None]
    quantities = [
        source_partials[left_at] * source_partials[right_at] for left_at, right_at in source_pairs
    ]
    quantities = quantities + [source_partials[param_at] * prefit_resid for param_at in range(5)]
    stacked = jnp.stack(quantities).reshape(20, blocks, SLOT_BLK)
    block_sums = jnp.einsum(
        "qbs,bsk->qbk", stacked, member, precision=lax.Precision.HIGHEST
    ).reshape(20, blocks * SRC_BLK)
    matrix = symmetric([block_sums[index_lookup] for index_lookup in range(15)], source_pairs, 5)
    source_update = jnp.stack(
        spd_solve(matrix, [block_sums[15 + param_at] for param_at in range(5)])
    )
    update_at_obs = jnp.einsum(
        "pbk,bsk->pbs",
        source_update.reshape(5, blocks, SRC_BLK),
        member,
        precision=lax.Precision.HIGHEST,
    ).reshape(5, count_obs)
    resid_after = valid_mask * (prefit_resid - jnp.sum(source_partials * update_at_obs, axis=0))
    masked_cal = valid_mask * calib_partials
    cal_terms = [masked_cal[left_at] * masked_cal[right_at] for left_at, right_at in calib_pairs]
    cal_terms = cal_terms + [masked_cal[param_at] * resid_after for param_at in range(3)]
    no_range = jnp.zeros((count_obs,), jnp.int32)
    cal_partial = pair_sum(jnp.stack(cal_terms), no_range, 1, obs_unit, CAL).reshape(9, CAL)
    cal_summed = lax.psum(cal_partial, ("wide", "narrow"))
    share_size = CAL // groups
    cal_mine = lax.dynamic_slice_in_dim(
        cal_summed, lax.axis_index("narrow") * share_size, share_size, 1
    )
    cal_matrix = symmetric([cal_mine[index_lookup] for index_lookup in range(6)], calib_pairs, 3)
    cal_update = jnp.stack(spd_solve(cal_matrix, [cal_mine[6 + param_at] for param_at in range(3)]))
    weights = spline(spline_position)
    total_knots = knots_dev * ranges
    term_rows = (
        weights[:, None, :] * attitude_partials[None, :, :] * resid_after[None, None, :]
    ).reshape(16, count_obs)
    totals = pair_sum(term_rows, obs_range, ranges, obs_knot, knots_dev).reshape(4, 4, total_knots)
    partial_rhs = shifted_knots(totals, total_knots)[:, :total_knots]
    own_rhs = lax.psum(
        lax.psum_scatter(partial_rhs, "wide", scatter_dimension=1, tiled=True), "narrow"
    )
    solution_vector = jnp.dot(
        given_inverse[0], own_rhs.reshape(4 * knots_dev), precision=lax.Precision.HIGHEST
    ).reshape(4, knots_dev)
    knot_gain = jnp.sqrt(1.0 - knot_decay * knot_decay)
    carry_mul, carry_add = lax.associative_scan(
        chain_step, (knot_decay, knot_gain * solution_vector), axis=1
    )
    entering = entering_2(
        (carry_mul[:, -1], carry_add[:, -1]),
        "wide",
        chain_step,
        (jnp.ones((4,), jnp.float32), jnp.zeros((4,), jnp.float32)),
    )
    attitude_update = carry_add + carry_mul * entering[1][:, None]
    return (source_update, attitude_update, cal_update)


def solution(mesh):
    placed = (
        P(("wide", "narrow")),
        P(None, ("wide", "narrow")),
        P(None, ("wide", "narrow")),
        P(("wide", "narrow")),
        P(None, ("wide", "narrow")),
        P(("wide", "narrow")),
        P(("wide", "narrow")),
        P(("wide", "narrow")),
        P(("wide", "narrow")),
        P(("wide", "narrow")),
        P("wide", None, None),
        P(None, "wide"),
    )
    return jax.shard_map(
        on_device,
        mesh=mesh,
        in_specs=placed,
        out_specs=(P(None, ("wide", "narrow")), P(None, "wide"), P(None, "narrow")),
        check_vma=False,
    )
```

profile of v0, /device:TPU:0, one launch (start us, length us, event | category | flops | bytes accessed | tf_op | source)
XLA Modules:
  0.0 486.0 jit_solution(6993398946896875538)
XLA Ops:
  8.1 5.9 %fusion.56 = (f32[1,40960]{1,0:T(1,128)S(1)}, f32[1,40960]{1,0:T(1,128)S(1)}, f32[1,40960]{1,0:T(1,128)S(1)}, f32[1,40960]{1,0:T(1,128)S(1)}, f32[1,40960]{1,0:T...) fusion(f32[5,40960]{1,0:T(8,128)} %param.19), kind=kLoop, calls=%fused_computation.198 | loop fusion | flops 450560 | bytes 2785280 | tf_op jit(solution)/shard_map/slice | solution.py:149
  20.0 12.1 %stack.132 = f32[20,64,640]{2,0,1:T(8,128)} concatenate(f32[1,64,640]{2,0,1:T(1,128)S(1)} %bitcast.132, f32[1,64,640]{2,0,1:T(1,128)S(1)} %bitcast.133, f32[1,64,640]{2,0,1:T(1,128)S(1)} %bitcast.135, f32[1,64,640]{2,0,1:T(1,128)} %bitcast.138, f32[1,64,640]{2,0,1:T(1,128)} %bitcast.142, f32[1,64,640]{2,0,1:T(1,128)S(1)} %bitcast.134, f32[1,64,640]{2,0,1:T(1,128)S(1)} %bitcast.136, ...), dimensions={0} | concatenate | bytes 6553600 | tf_op jit(solution)/shard_map/stack | solution.py:152
  32.2 26.6 %fusion.21 = f32[64,128,20]{1,2,0:T(8,128)S(1)} fusion(f32[20,64,640]{2,0,1:T(8,128)} %stack.132, f32[64,640]{1,0:T(8,128)S(1)} %copy-done.4, s32[64,640]{1,0:T(8,128)S(1)} %copy-done.6), kind=kOutput, calls=%fused_computation.26 | convolution fusion | flops 1268776960 | bytes 4259840 | tf_op jit(solution)/shard_map/qbs,bsk->qbk/dot_general | solution.py:153
  60.5 38.2 %fusion.19 = f32[64,640,5]{1,2,0:T(8,128)S(1)} fusion(f32[64,640]{1,0:T(8,128)S(1)} %copy-done.5, s32[64,640]{1,0:T(8,128)S(1)} %copy-done.7, f32[5,64,128]{2,1,0:T(8,128)S(1)} %constant_dynamic-update-slice_fusion), kind=kOutput, calls=%fused_computation.24 | convolution fusion | flops 325058560 | bytes 1310720 | tf_op jit(solution)/shard_map/pbk,bsk->pbs/dot_general | solution.py:160
  102.9 6.2 %stack.143 = f32[9,40960]{1,0:T(8,128)S(1)} concatenate(f32[1,40960]{1,0:T(1,128)} %get-tuple-element.477, f32[1,40960]{1,0:T(1,128)} %get-tuple-element.478, f32[1,40960]{1,0:T(1,128)} %get-tuple-element.480, f32[1,40960]{1,0:T(1,128)} %get-tuple-element.479, f32[1,40960]{1,0:T(1,128)} %get-tuple-element.481, f32[1,40960]{1,0:T(1,128)} %get-tuple-element.482, ...), dimensions={0} | concatenate | bytes 2949120 | tf_op jit(solution)/shard_map/stack | solution.py:171
  109.1 151.3 %while.44 = (s32[]{:T(128)}, f32[9,2016]{1,0:T(8,128)}, f32[9,40960]{1,0:T(8,128)S(1)}, s32[40960]{0:T(1024)}, s32[]{:T(128)}, /*index=5*/s32[]{:T(128)}, s32[]{:T(128)}, s32[]{:T(128)}) while((s32[]{:T(128)}, f32[9,2016]{1,0:T(8,128)}, f32[9,40960]{1,0:T(8,128)S(1)}, s32[40960]{0:T(1024)}, s32[]{:T(128)}, /*index=5*/s32[]{:T(128)}, ...), condition=%wide.region_8.9_spmd.clone, body=%wide.region_7.8_spmd.clone.sunk | while | flops 450072000 | bytes 300949 | solution.py:108
  109.8 6.0 %fusion.83 = f32[9,2016]{1,0:T(8,128)} fusion(s32[2048]{0:T(1024)S(1)} %dynamic_slice.78, f32[9,2016]{1,0:T(8,128)} %get-tuple-element.702, f32[9,40960]{1,0:T(8,128)S(1)} %get-tuple-element.711, s32[]{:T(128)S(6)} %select_n.56, pred[]{:T(512)S(6)} %compare.47), kind=kOutput, calls=%fused_computation.21.clone.1 | convolution fusion | flops 450072000 | bytes 284421 | tf_op jit(solution)/shard_map/while/body/eval_jaxpr/dot_general | solution.py:106
  116.5 6.9 %fusion.83 = f32[9,2016]{1,0:T(8,128)} fusion(s32[2048]{0:T(1024)S(1)} %dynamic_slice.78, f32[9,2016]{1,0:T(8,128)} %get-tuple-element.702, f32[9,40960]{1,0:T(8,128)S(1)} %get-tuple-element.711, s32[]{:T(128)S(6)} %select_n.56, pred[]{:T(512)S(6)} %compare.47), kind=kOutput, calls=%fused_computation.21.clone.1 | convolution fusion | flops 450072000 | bytes 284421 | tf_op jit(solution)/shard_map/while/body/eval_jaxpr/dot_general | solution.py:106
  124.1 6.9 %fusion.83 = f32[9,2016]{1,0:T(8,128)} fusion(s32[2048]{0:T(1024)S(1)} %dynamic_slice.78, f32[9,2016]{1,0:T(8,128)} %get-tuple-element.702, f32[9,40960]{1,0:T(8,128)S(1)} %get-tuple-element.711, s32[]{:T(128)S(6)} %select_n.56, pred[]{:T(512)S(6)} %compare.47), kind=kOutput, calls=%fused_computation.21.clone.1 | convolution fusion | flops 450072000 | bytes 284421 | tf_op jit(solution)/shard_map/while/body/eval_jaxpr/dot_general | solution.py:106
  131.7 6.9 %fusion.83 = f32[9,2016]{1,0:T(8,128)} fusion(s32[2048]{0:T(1024)S(1)} %dynamic_slice.78, f32[9,2016]{1,0:T(8,128)} %get-tuple-element.702, f32[9,40960]{1,0:T(8,128)S(1)} %get-tuple-element.711, s32[]{:T(128)S(6)} %select_n.56, pred[]{:T(512)S(6)} %compare.47), kind=kOutput, calls=%fused_computation.21.clone.1 | convolution fusion | flops 450072000 | bytes 284421 | tf_op jit(solution)/shard_map/while/body/eval_jaxpr/dot_general | solution.py:106
  139.3 6.9 %fusion.83 = f32[9,2016]{1,0:T(8,128)} fusion(s32[2048]{0:T(1024)S(1)} %dynamic_slice.78, f32[9,2016]{1,0:T(8,128)} %get-tuple-element.702, f32[9,40960]{1,0:T(8,128)S(1)} %get-tuple-element.711, s32[]{:T(128)S(6)} %select_n.56, pred[]{:T(512)S(6)} %compare.47), kind=kOutput, calls=%fused_computation.21.clone.1 | convolution fusion | flops 450072000 | bytes 284421 | tf_op jit(solution)/shard_map/while/body/eval_jaxpr/dot_general | solution.py:106
  146.9 6.9 %fusion.83 = f32[9,2016]{1,0:T(8,128)} fusion(s32[2048]{0:T(1024)S(1)} %dynamic_slice.78, f32[9,2016]{1,0:T(8,128)} %get-tuple-element.702, f32[9,40960]{1,0:T(8,128)S(1)} %get-tuple-element.711, s32[]{:T(128)S(6)} %select_n.56, pred[]{:T(512)S(6)} %compare.47), kind=kOutput, calls=%fused_computation.21.clone.1 | convolution fusion | flops 450072000 | bytes 284421 | tf_op jit(solution)/shard_map/while/body/eval_jaxpr/dot_general | solution.py:106
  154.6 6.9 %fusion.83 = f32[9,2016]{1,0:T(8,128)} fusion(s32[2048]{0:T(1024)S(1)} %dynamic_slice.78, f32[9,2016]{1,0:T(8,128)} %get-tuple-element.702, f32[9,40960]{1,0:T(8,128)S(1)} %get-tuple-element.711, s32[]{:T(128)S(6)} %select_n.56, pred[]{:T(512)S(6)} %compare.47), kind=kOutput, calls=%fused_computation.21.clone.1 | convolution fusion | flops 450072000 | bytes 284421 | tf_op jit(solution)/shard_map/while/body/eval_jaxpr/dot_general | solution.py:106
  162.2 6.9 %fusion.83 = f32[9,2016]{1,0:T(8,128)} fusion(s32[2048]{0:T(1024)S(1)} %dynamic_slice.78, f32[9,2016]{1,0:T(8,128)} %get-tuple-element.702, f32[9,40960]{1,0:T(8,128)S(1)} %get-tuple-element.711, s32[]{:T(128)S(6)} %select_n.56, pred[]{:T(512)S(6)} %compare.47), kind=kOutput, calls=%fused_computation.21.clone.1 | convolution fusion | flops 450072000 | bytes 284421 | tf_op jit(solution)/shard_map/while/body/eval_jaxpr/dot_general | solution.py:106
  169.8 6.9 %fusion.83 = f32[9,2016]{1,0:T(8,128)} fusion(s32[2048]{0:T(1024)S(1)} %dynamic_slice.78, f32[9,2016]{1,0:T(8,128)} %get-tuple-element.702, f32[9,40960]{1,0:T(8,128)S(1)} %get-tuple-element.711, s32[]{:T(128)S(6)} %select_n.56, pred[]{:T(512)S(6)} %compare.47), kind=kOutput, calls=%fused_computation.21.clone.1 | convolution fusion | flops 450072000 | bytes 284421 | tf_op jit(solution)/shard_map/while/body/eval_jaxpr/dot_general | solution.py:106
  177.4 6.9 %fusion.83 = f32[9,2016]{1,0:T(8,128)} fusion(s32[2048]{0:T(1024)S(1)} %dynamic_slice.78, f32[9,2016]{1,0:T(8,128)} %get-tuple-element.702, f32[9,40960]{1,0:T(8,128)S(1)} %get-tuple-element.711, s32[]{:T(128)S(6)} %select_n.56, pred[]{:T(512)S(6)} %compare.47), kind=kOutput, calls=%fused_computation.21.clone.1 | convolution fusion | flops 450072000 | bytes 284421 | tf_op jit(solution)/shard_map/while/body/eval_jaxpr/dot_general | solution.py:106
  185.0 6.9 %fusion.83 = f32[9,2016]{1,0:T(8,128)} fusion(s32[2048]{0:T(1024)S(1)} %dynamic_slice.78, f32[9,2016]{1,0:T(8,128)} %get-tuple-element.702, f32[9,40960]{1,0:T(8,128)S(1)} %get-tuple-element.711, s32[]{:T(128)S(6)} %select_n.56, pred[]{:T(512)S(6)} %compare.47), kind=kOutput, calls=%fused_computation.21.clone.1 | convolution fusion | flops 450072000 | bytes 284421 | tf_op jit(solution)/shard_map/while/body/eval_jaxpr/dot_general | solution.py:106
  192.6 6.9 %fusion.83 = f32[9,2016]{1,0:T(8,128)} fusion(s32[2048]{0:T(1024)S(1)} %dynamic_slice.78, f32[9,2016]{1,0:T(8,128)} %get-tuple-element.702, f32[9,40960]{1,0:T(8,128)S(1)} %get-tuple-element.711, s32[]{:T(128)S(6)} %select_n.56, pred[]{:T(512)S(6)} %compare.47), kind=kOutput, calls=%fused_computation.21.clone.1 | convolution fusion | flops 450072000 | bytes 284421 | tf_op jit(solution)/shard_map/while/body/eval_jaxpr/dot_general | solution.py:106
  200.2 6.9 %fusion.83 = f32[9,2016]{1,0:T(8,128)} fusion(s32[2048]{0:T(1024)S(1)} %dynamic_slice.78, f32[9,2016]{1,0:T(8,128)} %get-tuple-element.702, f32[9,40960]{1,0:T(8,128)S(1)} %get-tuple-element.711, s32[]{:T(128)S(6)} %select_n.56, pred[]{:T(512)S(6)} %compare.47), kind=kOutput, calls=%fused_computation.21.clone.1 | convolution fusion | flops 450072000 | bytes 284421 | tf_op jit(solution)/shard_map/while/body/eval_jaxpr/dot_general | solution.py:106
  207.8 6.9 %fusion.83 = f32[9,2016]{1,0:T(8,128)} fusion(s32[2048]{0:T(1024)S(1)} %dynamic_slice.78, f32[9,2016]{1,0:T(8,128)} %get-tuple-element.702, f32[9,40960]{1,0:T(8,128)S(1)} %get-tuple-element.711, s32[]{:T(128)S(6)} %select_n.56, pred[]{:T(512)S(6)} %compare.47), kind=kOutput, calls=%fused_computation.21.clone.1 | convolution fusion | flops 450072000 | bytes 284421 | tf_op jit(solution)/shard_map/while/body/eval_jaxpr/dot_general | solution.py:106
  215.4 6.9 %fusion.83 = f32[9,2016]{1,0:T(8,128)} fusion(s32[2048]{0:T(1024)S(1)} %dynamic_slice.78, f32[9,2016]{1,0:T(8,128)} %get-tuple-element.702, f32[9,40960]{1,0:T(8,128)S(1)} %get-tuple-element.711, s32[]{:T(128)S(6)} %select_n.56, pred[]{:T(512)S(6)} %compare.47), kind=kOutput, calls=%fused_computation.21.clone.1 | convolution fusion | flops 450072000 | bytes 284421 | tf_op jit(solution)/shard_map/while/body/eval_jaxpr/dot_general | solution.py:106
  223.0 6.9 %fusion.83 = f32[9,2016]{1,0:T(8,128)} fusion(s32[2048]{0:T(1024)S(1)} %dynamic_slice.78, f32[9,2016]{1,0:T(8,128)} %get-tuple-element.702, f32[9,40960]{1,0:T(8,128)S(1)} %get-tuple-element.711, s32[]{:T(128)S(6)} %select_n.56, pred[]{:T(512)S(6)} %compare.47), kind=kOutput, calls=%fused_computation.21.clone.1 | convolution fusion | flops 450072000 | bytes 284421 | tf_op jit(solution)/shard_map/while/body/eval_jaxpr/dot_general | solution.py:106
  230.7 6.9 %fusion.83 = f32[9,2016]{1,0:T(8,128)} fusion(s32[2048]{0:T(1024)S(1)} %dynamic_slice.78, f32[9,2016]{1,0:T(8,128)} %get-tuple-element.702, f32[9,40960]{1,0:T(8,128)S(1)} %get-tuple-element.711, s32[]{:T(128)S(6)} %select_n.56, pred[]{:T(512)S(6)} %compare.47), kind=kOutput, calls=%fused_computation.21.clone.1 | convolution fusion | flops 450072000 | bytes 284421 | tf_op jit(solution)/shard_map/while/body/eval_jaxpr/dot_general | solution.py:106
  238.3 6.9 %fusion.83 = f32[9,2016]{1,0:T(8,128)} fusion(s32[2048]{0:T(1024)S(1)} %dynamic_slice.78, f32[9,2016]{1,0:T(8,128)} %get-tuple-element.702, f32[9,40960]{1,0:T(8,128)S(1)} %get-tuple-element.711, s32[]{:T(128)S(6)} %select_n.56, pred[]{:T(512)S(6)} %compare.47), kind=kOutput, calls=%fused_computation.21.clone.1 | convolution fusion | flops 450072000 | bytes 284421 | tf_op jit(solution)/shard_map/while/body/eval_jaxpr/dot_general | solution.py:106
  245.9 6.9 %fusion.83 = f32[9,2016]{1,0:T(8,128)} fusion(s32[2048]{0:T(1024)S(1)} %dynamic_slice.78, f32[9,2016]{1,0:T(8,128)} %get-tuple-element.702, f32[9,40960]{1,0:T(8,128)S(1)} %get-tuple-element.711, s32[]{:T(128)S(6)} %select_n.56, pred[]{:T(512)S(6)} %compare.47), kind=kOutput, calls=%fused_computation.21.clone.1 | convolution fusion | flops 450072000 | bytes 284421 | tf_op jit(solution)/shard_map/while/body/eval_jaxpr/dot_general | solution.py:106
  253.5 6.9 %fusion.83 = f32[9,2016]{1,0:T(8,128)} fusion(s32[2048]{0:T(1024)S(1)} %dynamic_slice.78, f32[9,2016]{1,0:T(8,128)} %get-tuple-element.702, f32[9,40960]{1,0:T(8,128)S(1)} %get-tuple-element.711, s32[]{:T(128)S(6)} %select_n.56, pred[]{:T(512)S(6)} %compare.47), kind=kOutput, calls=%fused_computation.21.clone.1 | convolution fusion | flops 450072000 | bytes 284421 | tf_op jit(solution)/shard_map/while/body/eval_jaxpr/dot_general | solution.py:106
  269.5 97.1 %while.42 = (s32[]{:T(128)}, f32[128,256]{1,0:T(8,128)}, f32[16,40960]{1,0:T(8,128)}, s32[40960]{0:T(1024)}, s32[40960]{0:T(1024)}, /*index=5*/s32[]{:T(128)}, s32[]{:T(128)}, s32[]{:T(128)}, s32[]{:T(128)}) while((s32[]{:T(128)}, f32[128,256]{1,0:T(8,128)}, f32[16,40960]{1,0:T(8,128)}, s32[40960]{0:T(1024)}, s32[40960]{0:T(1024)}, ...), condition=%wide.region_2.0_spmd.clone, body=%wide.region_1.0_spmd.clone.sunk | while | flops 806191104 | bytes 835745 | solution.py:108
  373.6 12.3 %all-reduce.41.cloned.1.call-done = f32[9,2016]{1,0:T(8,128)} async-done(((f32[9,2016]{1,0:T(8,128)}), f32[9,2016]{1,0:T(8,128)}) %all-reduce.41.cloned.1.call-update) | async-done | bytes 72592 | tf_op jit(solution)/shard_map/psum | solution.py:172
  389.5 46.0 %reduce-scatter.4.cloned.1.call-done = f32[256,4]{1,0:T(8,128)} async-done(((f32[2048,4]{1,0:T(8,128)}), f32[256,4]{1,0:T(8,128)}) %reduce-scatter.4.cloned.1.call-update) | async-done | bytes 4112
  436.4 5.7 %psum.14 = f32[1024]{0:T(1024)S(1)} all-reduce(f32[1024]{0:T(1024)S(1)} %bitcast.179), channel_id=1, replica_groups=mesh['wide'=8,'narrow'=4] {'narrow'}, use_global_device_ids=true, to_apply=%region_4.0 | all-reduce | flops 1024 | bytes 8192 | tf_op jit(solution)/shard_map/psum | solution.py:186
  442.1 5.6 %fusion.64 = f32[1,4,256]{2,0,1:T(1,128)S(1)} fusion(f32[1024,1,1]{0,1,2:T(1,128)S(1)} %bitcast.180, f32[4,256,1024]{2,1,0:T(8,128)} %bitcast.105), kind=kOutput, calls=%fused_computation.206 | convolution fusion | flops 12582912 | bytes 4202496 | tf_op jit(solution)/shard_map/dot_general | solution.py:189
  458.1 19.4 %all-reduce.38 = (f32[32]{0:T(128)S(1)}, f32[32]{0:T(128)S(1)}) all-reduce(f32[32]{0:T(128)S(1)} %dynamic-update-slice, f32[32]{0:T(128)S(1)} %dynamic-update-slice.1), channel_id=2, replica_groups=mesh['wide'=8,'narrow'=4] {'wide'}, use_global_device_ids=true, to_apply=%add.36 | all-reduce | flops 64 | bytes 512
  (347 shorter events, 153.8 us)
Async XLA Ops:
  8.0 10.5 %copy-start.21 = (s32[64]{0:T(128)S(1)}, s32[64]{0:T(128)}, u32[]{:S(2)}) copy-start(s32[64]{0:T(128)} %param.24) | copy-start | bytes 772
  8.0 11.2 %copy-start.3 = (s32[40960]{0:T(1024)S(1)}, s32[40960]{0:T(1024)}, u32[]{:S(2)}) copy-start(s32[40960]{0:T(1024)} %param.23) | copy-start | bytes 491524
  8.0 11.9 %copy-start.2 = (f32[40960]{0:T(1024)S(1)}, f32[40960]{0:T(1024)}, u32[]{:S(2)}) copy-start(f32[40960]{0:T(1024)} %param.18) | copy-start | bytes 491524
  8.0 377.9 %all-reduce.41.cloned.1.call-start = ((), (), s32[]{:S(2)}) async-start(), calls=%async_computation.1 | async-start | bytes 262144 | tf_op jit(solution)/shard_map/psum | solution.py:172
  20.0 12.2 %copy-start.4 = (f32[64,640]{1,0:T(8,128)S(1)}, f32[64,640]{1,0:T(8,128)}, u32[]{:S(2)}) copy-start(f32[64,640]{1,0:T(8,128)} %get-tuple-element.555) | copy-start | bytes 491524
  20.0 12.2 %copy-start.6 = (s32[64,640]{1,0:T(8,128)S(1)}, s32[64,640]{1,0:T(8,128)}, u32[]{:S(2)}) copy-start(s32[64,640]{1,0:T(8,128)} %eq.114) | copy-start | bytes 491524
  58.7 1.7 copy-start.5
  58.7 1.7 copy-start.7
  60.5 38.3 %copy-start = (f32[5,40960]{1,0:T(8,128)S(1)}, f32[5,40960]{1,0:T(8,128)}, u32[]{:S(2)}) copy-start(f32[5,40960]{1,0:T(8,128)} %param.19) | copy-start | bytes 2457604
  60.5 38.9 %copy-start.1 = (f32[3,40960]{1,0:T(4,128)S(1)}, f32[3,40960]{1,0:T(4,128)}, u32[]{:S(2)}) copy-start(f32[3,40960]{1,0:T(4,128)} %param.22) | copy-start | bytes 1474564
  260.4 175.0 %reduce-scatter.4.cloned.1.call-start = ((), (), s32[]{:S(2)}) async-start(), calls=%async_computation.2 | async-start | bytes 1179648
  269.4 99.7 %copy-start.20 = (f32[4,256]{1,0:T(4,128)S(1)}, f32[4,256]{1,0:T(4,128)}, u32[]{:S(2)}) copy-start(f32[4,256]{1,0:T(4,128)} %param.29) | copy-start | bytes 12292
  269.4 100.4 %copy-start.22 = (u32[32]{0:T(128)S(1)}, u32[32]{0:T(128)}, u32[]{:S(2)}) copy-start(u32[32]{0:T(128)} %constant.194) | copy-start | bytes 388
  269.4 101.7 %copy-start.12 = (f32[1,64,128]{2,1,0:T(8,128)S(1)}, f32[1,64,128]{2,1,0:T(8,128)}, u32[]{:S(2)}) copy-start(f32[1,64,128]{2,1,0:T(8,128)} %get-tuple-element.491) | copy-start | bytes 98308
  269.4 101.7 %copy-start.13 = (f32[1,64,128]{2,1,0:T(8,128)S(1)}, f32[1,64,128]{2,1,0:T(8,128)}, u32[]{:S(2)}) copy-start(f32[1,64,128]{2,1,0:T(8,128)} %get-tuple-element.492) | copy-start | bytes 98308
  269.4 101.7 %copy-start.14 = (f32[1,64,128]{2,1,0:T(8,128)S(1)}, f32[1,64,128]{2,1,0:T(8,128)}, u32[]{:S(2)}) copy-start(f32[1,64,128]{2,1,0:T(8,128)} %get-tuple-element.493) | copy-start | bytes 98308
  269.4 101.7 %copy-start.15 = (f32[1,64,128]{2,1,0:T(8,128)S(1)}, f32[1,64,128]{2,1,0:T(8,128)}, u32[]{:S(2)}) copy-start(f32[1,64,128]{2,1,0:T(8,128)} %get-tuple-element.494) | copy-start | bytes 98308
  269.4 101.7 %copy-start.16 = (f32[1,64,128]{2,1,0:T(8,128)S(1)}, f32[1,64,128]{2,1,0:T(8,128)}, u32[]{:S(2)}) copy-start(f32[1,64,128]{2,1,0:T(8,128)} %get-tuple-element.495) | copy-start | bytes 98308
  269.5 101.7 %copy-start.17 = (f32[1,64,128]{2,1,0:T(8,128)S(1)}, f32[1,64,128]{2,1,0:T(8,128)}, u32[]{:S(2)}) copy-start(f32[1,64,128]{2,1,0:T(8,128)} %get-tuple-element.496) | copy-start | bytes 98308
  269.5 101.7 %copy-start.18 = (f32[1,64,128]{2,1,0:T(8,128)S(1)}, f32[1,64,128]{2,1,0:T(8,128)}, u32[]{:S(2)}) copy-start(f32[1,64,128]{2,1,0:T(8,128)} %get-tuple-element.497) | copy-start | bytes 98308
  269.5 101.7 %copy-start.19 = (f32[1,64,128]{2,1,0:T(8,128)S(1)}, f32[1,64,128]{2,1,0:T(8,128)}, u32[]{:S(2)}) copy-start(f32[1,64,128]{2,1,0:T(8,128)} %get-tuple-element.498) | copy-start | bytes 98308
  366.6 5.2 %copy-start.8 = (f32[1,64,128]{2,1,0:T(8,128)S(1)}, f32[1,64,128]{2,1,0:T(8,128)}, u32[]{:S(2)}) copy-start(f32[1,64,128]{2,1,0:T(8,128)} %get-tuple-element.489) | copy-start | bytes 98308
  366.6 5.2 %copy-start.9 = (f32[1,64,128]{2,1,0:T(8,128)S(1)}, f32[1,64,128]{2,1,0:T(8,128)}, u32[]{:S(2)}) copy-start(f32[1,64,128]{2,1,0:T(8,128)} %get-tuple-element.490) | copy-start | bytes 98308
  366.6 5.2 %copy-start.10 = (f32[1,64,128]{2,1,0:T(8,128)S(1)}, f32[1,64,128]{2,1,0:T(8,128)}, u32[]{:S(2)}) copy-start(f32[1,64,128]{2,1,0:T(8,128)} %get-tuple-element.487) | copy-start | bytes 98308
  366.6 5.2 %copy-start.11 = (f32[1,64,128]{2,1,0:T(8,128)S(1)}, f32[1,64,128]{2,1,0:T(8,128)}, u32[]{:S(2)}) copy-start(f32[1,64,128]{2,1,0:T(8,128)} %get-tuple-element.488) | copy-start | bytes 98308
  371.1 86.0 %slice-start = ((f32[4,256]{1,0:T(4,128)}), f32[4,1]{1,0:T(4,128)S(1)}, s32[]{:S(2)}) async-start(f32[4,256]{1,0:T(4,128)} %param.29), calls=%async_computation.3 | async-start | bytes 4096 | tf_op jit(solution)/shard_map/slice | solution.py:193
Sparse Core Ops, SparseCore 0:
  260.5 125.3 all-reduce.40
Sparse Core Ops, SparseCore 1:
  369.2 66.2 reduce-scatter.3
where the time goes:
time: 491 us; the launch traced here: 486 us
  matrix products  258 us (53%)
  local copies, waits for them, and re-layouts  95.9 us (20%)
  waiting for transfers between devices  58.3 us (12%)
  other arithmetic  31.2 us (6%)
  blocking collectives  25 us (5%)
  between operations  16.9 us (3%)
    dot_general x40, matrix products, accumulate(): jnp.dot(left_rows, second_hot, precision=lax.Precision.HIGHEST)  188 us
    unnamed x3, waiting for transfers between devices  46 us
    dot_general x1, matrix products, on_device(): jnp.einsum('pbk,bsk->pbs', source_update.reshape(5, blocks, SRC_BLK), mem...  38.2 us
    dynamic_slice x40, local copies, waits for them, and re-layouts, accumulate(): lax.dynamic_slice_in_dim(second_ids, starting_offset, piece_size, 0)  28 us
    dot_general x1, matrix products, on_device(): jnp.einsum('qbs,bsk->qbk', stacked, member, precision=lax.Precision.HIGHEST)  26.6 us
    unnamed x1, blocking collectives  19.4 us
    dynamic_slice x20, local copies, waits for them, and re-layouts, accumulate(): lax.dynamic_slice_in_dim(values, starting_offset, piece_size, 1)  18.3 us
    dynamic_slice x20, local copies, waits for them, and re-layouts, accumulate(): lax.dynamic_slice_in_dim(first_ids, starting_offset, piece_size, 0)  14.1 us
  transfers between devices with their start and end apart: 2, of which 2 were waited for; matrix products, arithmetic and copies ran while one was open for 24% of the time, Pallas kernels for 0%

commit v1 on v0

v1 whole, which is shorter than its diff:
```python
import functools

import jax
import jax.numpy as jnp
from jax import lax
from jax.experimental import pallas as pl
from jax.experimental.pallas import tpu as pltpu
from jax.sharding import PartitionSpec as P

SRC_BLK = 128
SLOT_BLK = 640
CAL = 2016
SPLIT = 4
ROWS = 24
NT = (((1,), (1,)), ((), ()))
F32 = jnp.float32
BF16 = jnp.bfloat16


def source_row(i, j):
    d = i - j
    return d * 8 + i if d <= 4 else 3 * 8 + j


def ldl_solve(matrix, target):
    n = len(target)
    low = [[None] * n for _ in range(n)]
    inv = [None] * n
    for c in range(n):
        scaled = [low[c][b][1] for b in range(c)]
        d = matrix(c, c) + 1.0
        for b in range(c):
            d = d - scaled[b] * low[c][b][0]
        inv[c] = 1.0 / d
        for r in range(c + 1, n):
            v = matrix(r, c)
            for b in range(c):
                v = v - low[r][b][1] * low[c][b][0]
            low[r][c] = (v * inv[c], v)
    z = []
    for r in range(n):
        v = target[r]
        for b in range(r):
            v = v - low[r][b][0] * z[b]
        z.append(v)
    x = [None] * n
    for r in reversed(range(n)):
        v = z[r] * inv[r]
        for b in range(r + 1, n):
            v = v - low[b][r][0] * x[b]
        x[r] = v
    return x


def split3(v):
    hi = v.astype(BF16).astype(F32)
    rest = v - hi
    mid = rest.astype(BF16).astype(F32)
    return hi, mid, rest - mid


def local_kernel(
    blocks, ranges, narrow,
    count_ref, resid_ref, sp_ref, att_ref, pos_ref, cal_ref, src_ref, rng_ref, knot_ref, unit_ref,
    update_ref, send_ref,
    e_ref, s_ref, x_ref, iota_ref, acc_att, acc_cal,
):
    iota_ref[...] = lax.broadcasted_iota(jnp.int32, (256, 128), 0).astype(F32).astype(BF16)
    slot = lax.broadcasted_iota(jnp.int32, (1, SLOT_BLK), 1)

    def normals(b, carry):
        at = pl.multiple_of(b * SLOT_BLK, 128)
        cols = pl.ds(at, SLOT_BLK)
        e = jnp.concatenate(
            [sp_ref[:, cols], resid_ref[:, cols], jnp.zeros((2, SLOT_BLK), F32)], axis=0
        )
        live = jnp.broadcast_to(slot < count_ref[b], (8, SLOT_BLK))
        e = jnp.where(live, e, 0.0)
        e_ref[:, cols] = e
        terms = jnp.concatenate(
            [e * e] + [e * pltpu.roll(e, d, axis=0) for d in range(1, 5)], axis=0
        )
        left = jnp.concatenate(split3(terms), axis=0).astype(BF16)
        src = src_ref[:, cols].astype(F32).astype(BF16)
        grid = jnp.concatenate([iota_ref[0:SRC_BLK, :]] * (SLOT_BLK // 128), axis=1)
        hot = jnp.where(grid == src, jnp.ones((), BF16), jnp.zeros((), BF16))
        sums = lax.dot_general(left, hot, NT, preferred_element_type=F32)
        s_ref[pl.ds(b, 40, stride=blocks), :] = sums[0:40] + sums[40:80] + sums[80:120]
        return carry

    lax.fori_loop(0, blocks, normals, 0, unroll=2)

    group = 16
    for g in range(0, blocks, group):
        def entry(i, j, g=g):
            row = source_row(i, j) * blocks + g
            return s_ref[row:row + group, :]

        x = ldl_solve(entry, [entry(5, j) for j in range(5)])
        for p in range(5):
            x_ref[pl.ds(g * 8 + p, group, stride=8), :] = x[p]
        x_ref[pl.ds(g * 8 + 5, group, stride=8), :] = jnp.full((group, 128), -1.0, F32)
        for p in (6, 7):
            x_ref[pl.ds(g * 8 + p, group, stride=8), :] = jnp.zeros((group, 128), F32)

    acc_att[...] = jnp.zeros_like(acc_att)
    acc_cal[...] = jnp.zeros_like(acc_cal)
    wide_slots = 2 * SLOT_BLK
    sub8 = lax.broadcasted_iota(jnp.int32, (8, wide_slots), 0)
    first = sub8 < 4
    per_row = 2 * (CAL // (narrow * SPLIT))

    def horner(u, low, high):
        c = [jnp.where(first, low[i], high[i]) for i in range(4)]
        return c[0] + u * (c[1] + u * (c[2] + u * c[3]))

    def rest(t, carry):
        at = pl.multiple_of(t * wide_slots, 128)
        cols = pl.ds(at, wide_slots)
        src = src_ref[:, cols]
        gathered = []
        for half in range(2):
            b = t * 2 + half
            table = x_ref[pl.ds(pl.multiple_of(b * 8, 8), 8), :]
            update_ref[:, pl.ds(pl.multiple_of(b * 128, 128), 128)] = table[0:5, :]
            for q in range(SLOT_BLK // 128):
                lo = half * SLOT_BLK + q * 128
                ids = jnp.broadcast_to(src[:, lo:lo + 128], (8, 128))
                gathered.append(jnp.take_along_axis(table, ids, axis=1, mode="promise_in_bounds"))
        prod = e_ref[:, cols] * jnp.concatenate(gathered, axis=1)
        prod = prod + pltpu.roll(prod, 4, axis=0)
        prod = prod + pltpu.roll(prod, 2, axis=0)
        prod = prod + pltpu.roll(prod, 1, axis=0)
        after = -prod

        u = jnp.broadcast_to(pos_ref[:, cols], (8, wide_slots))
        sixth = 1.0 / 6.0
        w01 = horner(u, (sixth, -0.5, 0.5, -sixth), (4.0 / 6.0, 0.0, -1.0, 0.5))
        w23 = horner(u, (sixth, 0.5, 0.5, -0.5), (0.0, 0.0, 0.0, sixth))
        att = att_ref[:, cols]
        scaled = jnp.concatenate([att, att], axis=0) * after
        terms = jnp.concatenate([scaled * w01, scaled * w23], axis=0)
        hi = terms.astype(BF16)
        pieces = jnp.concatenate([hi, (terms - hi.astype(F32)).astype(BF16)], axis=0)
        rng = jnp.broadcast_to(rng_ref[:, cols].astype(F32).astype(BF16), (32, wide_slots))
        zero = jnp.zeros((), BF16)
        one = jnp.ones((), BF16)
        left = jnp.concatenate(
            [jnp.where(rng == jnp.asarray(r, BF16), pieces, zero) for r in range(ranges)], axis=0
        )
        grid = jnp.concatenate([iota_ref[...]] * (wide_slots // 128), axis=1)
        knot = knot_ref[:, cols].astype(F32).astype(BF16)
        hot = jnp.where(grid == knot, one, zero)
        acc_att[...] += lax.dot_general(left, hot, NT, preferred_element_type=F32)

        slot2 = lax.broadcasted_iota(jnp.int32, (1, SLOT_BLK), 1)
        live = jnp.concatenate(
            [slot2 < count_ref[2 * t], slot2 < count_ref[2 * t + 1]], axis=1
        )
        cal = jnp.where(live, cal_ref[:, cols], 0.0)
        four = jnp.concatenate([cal, after[0:1, :]], axis=0)
        f = jnp.concatenate([four, four], axis=0)
        near = f * jnp.where(first, f, pltpu.roll(f, 1, axis=0))
        far = f * pltpu.roll(f, 2, axis=0)
        far_hi, far_mid, far_lo = split3(far)
        far = jnp.where(sub8 < 2, far_hi, jnp.where(first, far_mid, jnp.where(sub8 < 6, far_lo, 0.0)))
        pieces = jnp.concatenate(list(split3(near)) + [far], axis=0).astype(BF16)
        unit = unit_ref[:, cols]
        upper = (unit * ((1 << 22) // per_row + 1)) >> 22
        place = unit - upper * per_row
        place = place + jnp.where(place >= per_row // 2, 128 - per_row // 2, 0)
        upper = jnp.broadcast_to(upper.astype(F32).astype(BF16), (32, wide_slots))
        left = jnp.concatenate(
            [jnp.where(upper == jnp.asarray(r, BF16), pieces, zero) for r in range(narrow * SPLIT // 2)],
            axis=0,
        )
        hot = jnp.where(grid == place.astype(F32).astype(BF16), one, zero)
        acc_cal[...] += lax.dot_general(left, hot, NT, preferred_element_type=F32)
        return carry

    lax.fori_loop(0, blocks // 2, rest, 0)

    lane = lax.broadcasted_iota(jnp.int32, (4, 256), 1)
    cal_pieces = []
    for piece in range(narrow * SPLIT):
        top, half = piece // 2, (piece % 2) * 128
        part = acc_cal[top * 32:(top + 1) * 32, half:half + 128]
        near = part[0:8] + part[8:16] + part[16:24]
        far = part[24:26] + part[26:28] + part[28:30]
        cal_pieces.append((near, far))
    before = None
    for r in range(ranges):
        part = acc_att[r * 32:r * 32 + 16, :] + acc_att[r * 32 + 16:r * 32 + 32, :]
        rolled = [part[0:4]] + [pltpu.roll(part[4 * k:4 * k + 4], k, axis=1) for k in range(1, 4)]
        total = rolled[0]
        for k in range(1, 4):
            wrapped = jnp.zeros((4, 256), F32) if before is None else before[k]
            total = total + jnp.where(lane >= k, rolled[k], wrapped)
        before = rolled
        for n in range(narrow):
            d = r * narrow + n
            near, far = cal_pieces[n * SPLIT + r % SPLIT]
            send_ref[d, 0:4, :] = total[:, 0:128]
            send_ref[d, 4:8, :] = total[:, 128:256]
            send_ref[d, 8:16, :] = near
            send_ref[d, 16:18, :] = far
            send_ref[d, 18:24, :] = jnp.zeros((6, 128), F32)


def exchange_kernel(
    wide, narrow,
    send_ref, inverse_ref, decay_ref,
    att_out, cal_out,
    recv, g_ref, carry_buf, cal_buf,
    g_sem, send_sem, recv_sem, carry_send, carry_recv, cal_send, cal_recv,
):
    count = wide * narrow
    w = lax.axis_index("wide")
    n = lax.axis_index("narrow")
    me = w * narrow + n
    mesh_id = pl.DeviceIdType.MESH
    load = pltpu.make_async_copy(inverse_ref.at[0], g_ref, g_sem)
    load.start()

    barrier = pltpu.get_barrier_semaphore()

    def greet(i, c):
        d = lax.rem(me + i, count)
        pl.semaphore_signal(
            barrier, inc=1, device_id=(d // narrow, lax.rem(d, narrow)), device_id_type=mesh_id
        )
        return c

    lax.fori_loop(1, count, greet, 0)
    pl.semaphore_wait(barrier, count - 1)

    def block_copy(i, slot):
        d = lax.rem(me + i, count)
        return pltpu.make_async_remote_copy(
            src_ref=send_ref.at[d],
            dst_ref=recv.at[slot],
            send_sem=send_sem.at[i],
            recv_sem=recv_sem.at[slot],
            device_id=(d // narrow, lax.rem(d, narrow)),
            device_id_type=mesh_id,
        )

    def launch(i, c):
        block_copy(i, me).start()
        return c

    lax.fori_loop(1, count, launch, 0)

    def collect(i, total):
        s = lax.rem(me + count - i, count)
        block_copy(i, s).wait_recv()
        return total + recv[s]

    total = lax.fori_loop(1, count, collect, send_ref[me])

    near, far = total[8:16], total[16:18]
    pair = {
        (0, 0): near[0:1], (1, 1): near[1:2], (2, 2): near[2:3],
        (1, 0): near[5:6], (2, 1): near[6:7], (2, 0): far[0:1],
    }
    x = ldl_solve(lambda i, j: pair[(i, j)], [near[4:5], far[1:2], near[7:8]])
    base = (w // SPLIT) * SPLIT
    mine = lax.rem(w, SPLIT)
    cal_buf[mine] = jnp.concatenate(x + [jnp.zeros((5, 128), F32)], axis=0)

    def cal_copy(i, slot):
        to = lax.rem(mine + i, SPLIT)
        return pltpu.make_async_remote_copy(
            src_ref=cal_buf.at[mine],
            dst_ref=cal_buf.at[slot],
            send_sem=cal_send.at[i],
            recv_sem=cal_recv.at[slot],
            device_id=(base + to, n),
            device_id_type=mesh_id,
        )

    for i in range(1, SPLIT):
        cal_copy(i, mine).start()

    columns = total[0:8].T
    load.wait()
    y = jnp.zeros((8, 1024), F32)
    for r in range(8):
        at = (r % 4) * 256 + (r // 4) * 128
        prod = columns[:, r:r + 1] * g_ref[at:at + 128, :]
        for j in range(16):
            y = y + prod[j * 8:(j + 1) * 8]
    y = jnp.sum(y, axis=0, keepdims=True)
    value = jnp.concatenate([y[:, c * 256:(c + 1) * 256] for c in range(4)], axis=0)
    mul = decay_ref[...]
    add = jnp.sqrt(1.0 - mul * mul) * value
    lane = lax.broadcasted_iota(jnp.int32, (4, 256), 1)
    step = 1
    while step < 256:
        inside = lane >= step
        add = add + mul * jnp.where(inside, pltpu.roll(add, step, axis=1), 0.0)
        mul = mul * jnp.where(inside, pltpu.roll(mul, step, axis=1), 1.0)
        step *= 2
    carry_buf[w] = jnp.concatenate(
        [jnp.broadcast_to(mul[:, 255:256], (4, 128)), jnp.broadcast_to(add[:, 255:256], (4, 128))],
        axis=0,
    )

    def carry_copy(i, slot):
        to = lax.rem(w + i, wide)
        return pltpu.make_async_remote_copy(
            src_ref=carry_buf.at[w],
            dst_ref=carry_buf.at[slot],
            send_sem=carry_send.at[i],
            recv_sem=carry_recv.at[slot],
            device_id=(to, n),
            device_id_type=mesh_id,
        )

    for i in range(1, wide):
        carry_copy(i, w).start()
    for i in range(1, SPLIT):
        cal_copy(i, lax.rem(mine + SPLIT - i, SPLIT)).wait_recv()
    for j in range(SPLIT):
        cal_out[j] = cal_buf[j]
    for i in range(1, wide):
        carry_copy(i, lax.rem(w + wide - i, wide)).wait_recv()
    state = jnp.zeros((4, 128), F32)
    for p in range(wide):
        piece = carry_buf[p]
        state = jnp.where(p < w, piece[0:4] * state + piece[4:8], state)
    att_out[...] = add + mul * jnp.concatenate([state, state], axis=1)

    def drain(i, c):
        block_copy(i, me).wait_send()
        return c

    lax.fori_loop(1, count, drain, 0)
    for i in range(1, SPLIT):
        cal_copy(i, mine).wait_send()
    for i in range(1, wide):
        carry_copy(i, w).wait_send()


def on_device(
    prefit_resid, source_partials, attitude_partials, spline_position, calib_partials, obs_source,
    block_count, obs_range, obs_knot, obs_unit, given_inverse, knot_decay,
):
    wide = lax.axis_size("wide")
    narrow = lax.axis_size("narrow")
    blocks = block_count.shape[0]
    slots = prefit_resid.shape[0]
    count = wide * narrow
    vmem = pl.BlockSpec(memory_space=pltpu.VMEM)
    row = lambda v: v.reshape(1, slots)
    source_update, send = pl.pallas_call(
        functools.partial(local_kernel, blocks, wide, narrow),
        out_shape=(
            jax.ShapeDtypeStruct((5, blocks * SRC_BLK), F32),
            jax.ShapeDtypeStruct((count, ROWS, 128), F32),
        ),
        in_specs=[pl.BlockSpec(memory_space=pltpu.SMEM)] + [vmem] * 9,
        out_specs=(vmem, vmem),
        scratch_shapes=[
            pltpu.VMEM((8, slots), F32),
            pltpu.VMEM((40 * blocks, 128), F32),
            pltpu.VMEM((8 * blocks, 128), F32),
            pltpu.VMEM((256, 128), BF16),
            pltpu.VMEM((wide * 32, 256), F32),
            pltpu.VMEM((narrow * SPLIT // 2 * 32, 256), F32),
        ],
        compiler_params=pltpu.CompilerParams(vmem_limit_bytes=56 * 1024 * 1024),
        name="local_sums",
    )(
        block_count, row(prefit_resid), source_partials, attitude_partials, row(spline_position),
        calib_partials, row(obs_source), row(obs_range), row(obs_knot), row(obs_unit),
    )
    dma = pltpu.SemaphoreType.DMA
    attitude_update, cal = pl.pallas_call(
        functools.partial(exchange_kernel, wide, narrow),
        out_shape=(
            jax.ShapeDtypeStruct(knot_decay.shape, F32),
            jax.ShapeDtypeStruct((SPLIT, 8, 128), F32),
        ),
        in_specs=[vmem, pl.BlockSpec(memory_space=pl.ANY), vmem],
        out_specs=(vmem, vmem),
        scratch_shapes=[
            pltpu.VMEM((count, ROWS, 128), F32),
            pltpu.VMEM(given_inverse.shape[1:], F32),
            pltpu.VMEM((wide, 8, 128), F32),
            pltpu.VMEM((SPLIT, 8, 128), F32),
            dma,
            dma((count,)), dma((count,)),
            dma((wide,)), dma((wide,)),
            dma((SPLIT,)), dma((SPLIT,)),
        ],
        compiler_params=pltpu.CompilerParams(
            collective_id=0, has_side_effects=True, vmem_limit_bytes=32 * 1024 * 1024
        ),
        name="exchange",
    )(send, given_inverse, knot_decay)
    per = CAL // (narrow * SPLIT)
    cal_update = cal[:, 0:3, 0:per].transpose(1, 0, 2).reshape(3, SPLIT * per)
    return (source_update, attitude_update, cal_update)


def solution(mesh):
    both = P(("wide", "narrow"))
    rows = P(None, ("wide", "narrow"))
    placed = (
        both, rows, rows, both, rows, both, both, both, both, both, P("wide", None, None), P(None, "wide"),
    )
    return jax.shard_map(
        on_device,
        mesh=mesh,
        in_specs=placed,
        out_specs=(rows, P(None, "wide"), P(None, "narrow")),
        check_vma=False,
    )
```

time: 491 us -> 60.8 us (0.12)
  matrix products: 258 us -> 0 us
  local copies, waits for them, and re-layouts: 95.9 us -> 5.15 us
  waiting for transfers between devices: 58.3 us -> 0 us
  Pallas kernels: 0 us -> 54.7 us
  other arithmetic: 31.2 us -> 0 us
  blocking collectives: 25 us -> 0 us
  between operations: 16.9 us -> 0.66 us
    dot_general x43 -> x0, matrix products: 258 us -> none  [the longest x40 188 us: accumulate(): jnp.dot(left_rows, second_hot, precision=lax.Precision.HIGHEST)]
    dynamic_slice x80 -> x0, local copies, waits for them, and re-layouts: 60.5 us -> none  [the longest x40 28 us: accumulate(): lax.dynamic_slice_in_dim(second_ids, starting_offset, piece_size, 0)]
    pallas_call x0 -> x2, Pallas kernels: none -> 54.7 us  [the longest x1 30.5 us: on_device(): pl.pallas_call(functools.partial(local_kernel, blocks, wide, narrow), out...]
    unnamed x3 -> x0, waiting for transfers between devices: 46 us -> none
    unnamed x1 -> x0, blocking collectives: 19.4 us -> none
    another operation x4 -> x0, local copies, waits for them, and re-layouts: 19.3 us -> none  [the longest x1 12.1 us: on_device(): stacked = jnp.stack(quantities).reshape(20, blocks, SLOT_BLK)]
    slice x7 -> x0, other arithmetic: 12.7 us -> none  [the longest x2 10.4 us: on_device(): source_partials[right_at]]
    psum x1 -> x0, waiting for transfers between devices: 12.3 us -> none  [on_device(): cal_summed = lax.psum(cal_partial, ('wide', 'narrow'))]
  transfers between devices with their start and end apart: 2 -> 0, of which waited for: 2 -> 0; matrix products, arithmetic and copies ran while one was open for 24% -> 0% of each run, Pallas kernels for 0% -> 0%
where the time goes in v1:
time: 60.8 us; the launch traced here: 60.5 us
  Pallas kernels  54.7 us (90%)
  local copies, waits for them, and re-layouts  5.15 us (8%)
  between operations  0.66 us (1%)
    pallas_call x1, Pallas kernels, on_device(): pl.pallas_call(functools.partial(local_kernel, blocks, wide, narrow), out...  30.5 us
    pallas_call x1, Pallas kernels, on_device(): pl.pallas_call(functools.partial(exchange_kernel, wide, narrow), out_shap...  24.2 us
    unnamed x7, local copies, waits for them, and re-layouts  4.46 us

profile of v1, /device:TPU:0, one launch (start us, length us, event | category | flops | bytes accessed | tf_op | source)
XLA Modules:
  0.0 60.5 jit_solution(17927463751862670763)
XLA Ops:
  0.6 30.5 %local_sums.1 = (f32[5,8192]{1,0:T(8,128)}, f32[32,24,128]{2,1,0:T(8,128)}) custom-call(s32[64]{0:T(128)} %count_ref.1, f32[1,40960]{1,0:T(1,128)} %bitcast.8, f32[5,40960]{1,0:T(8,128)} %sp_ref.1, f32[4,40960]{1,0:T(4,128)} %att_ref.1, f32[1,40960]{1,0:T(1,128)} %bitcast.9, f32[3,40960]{1,0:T(4,128)} %cal_ref.1, s32[1,40960]{1,0:T(1,128)} %bitcast.10, ...), custom_call_target="tpu_custom_call" | custom-call | tf_op jit(solution)/shard_map/local_sums/pallas_call | solution.py:356
  31.2 0.0 copy-start
  31.2 2.2 %copy-done = f32[1,1024,1024]{2,1,0:T(8,128)S(1)} copy-done((f32[1,1024,1024]{2,1,0:T(8,128)S(1)}, f32[1,1024,1024]{2,1,0:T(8,128)}, u32[]{:S(2)}) %copy-start) | copy-done | bytes 4194328
  33.4 0.0 copy-start.1
  33.4 1.0 %copy-done.1 = f32[32,24,128]{2,1,0:T(8,128)S(1)} copy-done((f32[32,24,128]{2,1,0:T(8,128)S(1)}, f32[32,24,128]{2,1,0:T(8,128)}, u32[]{:S(2)}) %copy-start.1) | copy-done | bytes 393240
  34.4 0.0 copy-start.2
  34.4 0.7 %copy-done.2 = f32[4,256]{1,0:T(4,128)S(1)} copy-done((f32[4,256]{1,0:T(4,128)S(1)}, f32[4,256]{1,0:T(4,128)}, u32[]{:S(2)}) %copy-start.2) | copy-done | bytes 4120
  35.1 24.2 %exchange.1 = (f32[4,256]{1,0:T(4,128)S(1)}, f32[4,8,128]{2,1,0:T(8,128)S(1)}) custom-call(f32[32,24,128]{2,1,0:T(8,128)S(1)} %copy-done.1, f32[1,1024,1024]{2,1,0:T(8,128)S(1)} %copy-done, f32[4,256]{1,0:T(4,128)S(1)} %copy-done.2), custom_call_target="tpu_custom_call" | custom-call | tf_op jit(solution)/shard_map/exchange/pallas_call | solution.py:379
  59.3 0.7 %reshape.33 = f32[3,504]{1,0:T(4,128)} reshape(f32[3,4,126]{2,1,0:T(4,128)S(1)} %copy.15) | data formatting | bytes 12096 | tf_op jit(solution)/shard_map/reshape | solution.py:403
  59.9 0.6 copy.17
  (2 shorter events, 0.0 us)
Async XLA Ops:
  31.2 2.2 %copy-start = (f32[1,1024,1024]{2,1,0:T(8,128)S(1)}, f32[1,1024,1024]{2,1,0:T(8,128)}, u32[]{:S(2)}) copy-start(f32[1,1024,1024]{2,1,0:T(8,128)} %inverse_ref.1) | copy-start | bytes 12582916
  33.4 1.0 %copy-start.1 = (f32[32,24,128]{2,1,0:T(8,128)S(1)}, f32[32,24,128]{2,1,0:T(8,128)}, u32[]{:S(2)}) copy-start(f32[32,24,128]{2,1,0:T(8,128)} %get-tuple-element.8.send_ref) | copy-start | bytes 1179652
  34.4 0.7 %copy-start.2 = (f32[4,256]{1,0:T(4,128)S(1)}, f32[4,256]{1,0:T(4,128)}, u32[]{:S(2)}) copy-start(f32[4,256]{1,0:T(4,128)} %decay_ref.1) | copy-start | bytes 12292

commit v2 on v1

--- a/solution.py
+++ b/solution.py
@@ -10,8 +10,7 @@
 SRC_BLK = 128
 SLOT_BLK = 640
 CAL = 2016
-SPLIT = 4
-ROWS = 24
+SPLIT = 8
 NT = (((1,), (1,)), ((), ()))
 F32 = jnp.float32
 BF16 = jnp.bfloat16
@@ -61,12 +60,23 @@
 
 def local_kernel(
     blocks, ranges, narrow,
-    count_ref, resid_ref, sp_ref, att_ref, pos_ref, cal_ref, src_ref, rng_ref, knot_ref, unit_ref,
+    count_ref, resid_hbm, sp_hbm, src_hbm, att_hbm, pos_hbm, cal_hbm, rng_hbm, knot_hbm, unit_hbm,
     update_ref, send_ref,
     e_ref, s_ref, x_ref, iota_ref, acc_att, acc_cal,
+    resid_ref, sp_ref, src_ref, att_ref, pos_ref, cal_ref, rng_ref, knot_ref, unit_ref, sems,
 ):
+    moves = [
+        (resid_hbm, resid_ref), (sp_hbm, sp_ref), (src_hbm, src_ref),
+        (att_hbm, att_ref), (pos_hbm, pos_ref), (cal_hbm, cal_ref),
+        (rng_hbm, rng_ref), (knot_hbm, knot_ref), (unit_hbm, unit_ref),
+    ]
+    loads = [pltpu.make_async_copy(a, b, sems.at[k]) for k, (a, b) in enumerate(moves)]
+    for load in loads:
+        load.start()
     iota_ref[...] = lax.broadcasted_iota(jnp.int32, (256, 128), 0).astype(F32).astype(BF16)
     slot = lax.broadcasted_iota(jnp.int32, (1, SLOT_BLK), 1)
+    for load in loads[0:3]:
+        load.wait()
 
     def normals(b, carry):
         at = pl.multiple_of(b * SLOT_BLK, 128)
@@ -88,7 +98,7 @@
         s_ref[pl.ds(b, 40, stride=blocks), :] = sums[0:40] + sums[40:80] + sums[80:120]
         return carry
 
-    lax.fori_loop(0, blocks, normals, 0, unroll=2)
+    lax.fori_loop(0, blocks, normals, 0, unroll=4)
 
     group = 16
     for g in range(0, blocks, group):
@@ -103,12 +113,15 @@
         for p in (6, 7):
             x_ref[pl.ds(g * 8 + p, group, stride=8), :] = jnp.zeros((group, 128), F32)
 
+    for load in loads[3:9]:
+        load.wait()
     acc_att[...] = jnp.zeros_like(acc_att)
     acc_cal[...] = jnp.zeros_like(acc_cal)
     wide_slots = 2 * SLOT_BLK
     sub8 = lax.broadcasted_iota(jnp.int32, (8, wide_slots), 0)
     first = sub8 < 4
-    per_row = 2 * (CAL // (narrow * SPLIT))
+    per = CAL // (narrow * SPLIT)
+    per_row = 4 * per
 
     def horner(u, low, high):
         c = [jnp.where(first, low[i], high[i]) for i in range(4)]
@@ -142,11 +155,16 @@
         terms = jnp.concatenate([scaled * w01, scaled * w23], axis=0)
         hi = terms.astype(BF16)
         pieces = jnp.concatenate([hi, (terms - hi.astype(F32)).astype(BF16)], axis=0)
-        rng = jnp.broadcast_to(rng_ref[:, cols].astype(F32).astype(BF16), (32, wide_slots))
+        rng = jnp.broadcast_to(rng_ref[:, cols].astype(F32).astype(BF16), (16, wide_slots))
         zero = jnp.zeros((), BF16)
         one = jnp.ones((), BF16)
+
+        def masked(ids, r, parts):
+            here = ids == jnp.asarray(r, BF16)
+            return [jnp.where(here, parts[k:k + 16], zero) for k in (0, 16)]
+
         left = jnp.concatenate(
-            [jnp.where(rng == jnp.asarray(r, BF16), pieces, zero) for r in range(ranges)], axis=0
+            [v for r in range(ranges) for v in masked(rng, r, pieces)], axis=0
         )
         grid = jnp.concatenate([iota_ref[...]] * (wide_slots // 128), axis=1)
         knot = knot_ref[:, cols].astype(F32).astype(BF16)
@@ -168,26 +186,31 @@
         unit = unit_ref[:, cols]
         upper = (unit * ((1 << 22) // per_row + 1)) >> 22
         place = unit - upper * per_row
-        place = place + jnp.where(place >= per_row // 2, 128 - per_row // 2, 0)
-        upper = jnp.broadcast_to(upper.astype(F32).astype(BF16), (32, wide_slots))
+        late = [jnp.where(place >= q * per, 64 - per, 0) for q in range(1, 4)]
+        place = place + (late[0] + late[1] + late[2])
+        upper = jnp.broadcast_to(upper.astype(F32).astype(BF16), (16, wide_slots))
         left = jnp.concatenate(
-            [jnp.where(upper == jnp.asarray(r, BF16), pieces, zero) for r in range(narrow * SPLIT // 2)],
+            [v for r in range(narrow * 2) for v in masked(upper, r, pieces)],
             axis=0,
         )
         hot = jnp.where(grid == place.astype(F32).astype(BF16), one, zero)
         acc_cal[...] += lax.dot_general(left, hot, NT, preferred_element_type=F32)
         return carry
 
-    lax.fori_loop(0, blocks // 2, rest, 0)
+    lax.fori_loop(0, blocks // 2, rest, 0, unroll=2)
 
     lane = lax.broadcasted_iota(jnp.int32, (4, 256), 1)
     cal_pieces = []
-    for piece in range(narrow * SPLIT):
-        top, half = piece // 2, (piece % 2) * 128
+    low = lax.broadcasted_iota(jnp.int32, (5, 128), 1) < 64
+    for pair in range(narrow * SPLIT // 2):
+        top, half = pair // 2, (pair % 2) * 128
         part = acc_cal[top * 32:(top + 1) * 32, half:half + 128]
         near = part[0:8] + part[8:16] + part[16:24]
         far = part[24:26] + part[26:28] + part[28:30]
-        cal_pieces.append((near, far))
+        upper5 = near[0:5]
+        lower5 = jnp.concatenate([near[5:8], far], axis=0)
+        cal_pieces.append(jnp.where(low, upper5, pltpu.roll(lower5, 64, axis=1)))
+        cal_pieces.append(jnp.where(low, pltpu.roll(upper5, 64, axis=1), lower5))
     before = None
     for r in range(ranges):
         part = acc_att[r * 32:r * 32 + 16, :] + acc_att[r * 32 + 16:r * 32 + 32, :]
@@ -199,95 +222,83 @@
         before = rolled
         for n in range(narrow):
             d = r * narrow + n
-            near, far = cal_pieces[n * SPLIT + r % SPLIT]
-            send_ref[d, 0:4, :] = total[:, 0:128]
-            send_ref[d, 4:8, :] = total[:, 128:256]
-            send_ref[d, 8:16, :] = near
-            send_ref[d, 16:18, :] = far
-            send_ref[d, 18:24, :] = jnp.zeros((6, 128), F32)
+            send_ref[d, 0:1, :] = total[n:n + 1, 0:128]
+            send_ref[d, 1:2, :] = total[n:n + 1, 128:256]
+            send_ref[d, 2:7, :] = cal_pieces[n * SPLIT + r % SPLIT]
+            send_ref[d, 7:8, :] = jnp.zeros((1, 128), F32)
 
 
 def exchange_kernel(
     wide, narrow,
-    send_ref, inverse_ref, decay_ref,
+    send_ref, inverse_ref, decay_hbm,
     att_out, cal_out,
-    recv, g_ref, carry_buf, cal_buf,
-    g_sem, send_sem, recv_sem, carry_send, carry_recv, cal_send, cal_recv,
+    recv, mine_buf, recv2, g_ref, decay_ref,
+    send_sem, recv_sem, send_sem2, recv_sem2, local_sem,
 ):
-    count = wide * narrow
     w = lax.axis_index("wide")
     n = lax.axis_index("narrow")
     me = w * narrow + n
     mesh_id = pl.DeviceIdType.MESH
-    load = pltpu.make_async_copy(inverse_ref.at[0], g_ref, g_sem)
-    load.start()
+    own = pl.ds(pl.multiple_of(n * 256, 256), 256)
+    loads = [
+        pltpu.make_async_copy(send_ref.at[me], recv.at[me], local_sem.at[0]),
+        pltpu.make_async_copy(inverse_ref.at[0, own], g_ref, local_sem.at[1]),
+        pltpu.make_async_copy(decay_hbm, decay_ref, local_sem.at[2]),
+    ]
+    for load in loads:
+        load.start()
+
+    def others(visit, carry, sign):
+        ns = [lax.rem(n + (sign * dn) % narrow, narrow) for dn in range(narrow)]
+        for dn in range(1, narrow):
+            carry = visit(dn, w, ns[dn], carry)
+
+        def row(dw, carry):
+            to = lax.rem(w + wide + sign * dw, wide)
+            for dn in range(narrow):
+                carry = visit(dw * narrow + dn, to, ns[dn], carry)
+            return carry
+
+        return lax.fori_loop(1, wide, row, carry)
 
     barrier = pltpu.get_barrier_semaphore()
 
-    def greet(i, c):
-        d = lax.rem(me + i, count)
-        pl.semaphore_signal(
-            barrier, inc=1, device_id=(d // narrow, lax.rem(d, narrow)), device_id_type=mesh_id
-        )
+    def greet(i, tw, tn, c):
+        pl.semaphore_signal(barrier, inc=1, device_id=(tw, tn), device_id_type=mesh_id)
         return c
 
-    lax.fori_loop(1, count, greet, 0)
-    pl.semaphore_wait(barrier, count - 1)
-
-    def block_copy(i, slot):
-        d = lax.rem(me + i, count)
+    others(greet, 0, 1)
+    pl.semaphore_wait(barrier, wide * narrow - 1)
+
+    def first_copy(i, tw, tn, slot):
         return pltpu.make_async_remote_copy(
-            src_ref=send_ref.at[d],
+            src_ref=send_ref.at[tw * narrow + tn],
             dst_ref=recv.at[slot],
             send_sem=send_sem.at[i],
             recv_sem=recv_sem.at[slot],
-            device_id=(d // narrow, lax.rem(d, narrow)),
+            device_id=(tw, tn),
             device_id_type=mesh_id,
         )
 
-    def launch(i, c):
-        block_copy(i, me).start()
+    def first_start(i, tw, tn, c):
+        first_copy(i, tw, tn, me).start()
         return c
 
-    lax.fori_loop(1, count, launch, 0)
-
-    def collect(i, total):
-        s = lax.rem(me + count - i, count)
-        block_copy(i, s).wait_recv()
+    others(first_start, 0, 1)
+
+    def collect(i, tw, tn, total):
+        s = tw * narrow + tn
+        first_copy(i, tw, tn, s).wait_recv()
         return total + recv[s]
 
-    total = lax.fori_loop(1, count, collect, send_ref[me])
-
-    near, far = total[8:16], total[16:18]
-    pair = {
-        (0, 0): near[0:1], (1, 1): near[1:2], (2, 2): near[2:3],
-        (1, 0): near[5:6], (2, 1): near[6:7], (2, 0): far[0:1],
-    }
-    x = ldl_solve(lambda i, j: pair[(i, j)], [near[4:5], far[1:2], near[7:8]])
-    base = (w // SPLIT) * SPLIT
-    mine = lax.rem(w, SPLIT)
-    cal_buf[mine] = jnp.concatenate(x + [jnp.zeros((5, 128), F32)], axis=0)
-
-    def cal_copy(i, slot):
-        to = lax.rem(mine + i, SPLIT)
-        return pltpu.make_async_remote_copy(
-            src_ref=cal_buf.at[mine],
-            dst_ref=cal_buf.at[slot],
-            send_sem=cal_send.at[i],
-            recv_sem=cal_recv.at[slot],
-            device_id=(base + to, n),
-            device_id_type=mesh_id,
-        )
-
-    for i in range(1, SPLIT):
-        cal_copy(i, mine).start()
-
-    columns = total[0:8].T
-    load.wait()
+    for load in loads:
+        load.wait()
+    total = others(collect, recv[me], -1)
+
+    columns = total.T
     y = jnp.zeros((8, 1024), F32)
-    for r in range(8):
-        at = (r % 4) * 256 + (r // 4) * 128
-        prod = columns[:, r:r + 1] * g_ref[at:at + 128, :]
+    for r in range(2):
+        prod = columns[:, r:r + 1] * g_ref[r * 128:(r + 1) * 128, :]
         for j in range(16):
             y = y + prod[j * 8:(j + 1) * 8]
     y = jnp.sum(y, axis=0, keepdims=True)
@@ -301,45 +312,68 @@
         add = add + mul * jnp.where(inside, pltpu.roll(add, step, axis=1), 0.0)
         mul = mul * jnp.where(inside, pltpu.roll(mul, step, axis=1), 1.0)
         step *= 2
-    carry_buf[w] = jnp.concatenate(
-        [jnp.broadcast_to(mul[:, 255:256], (4, 128)), jnp.broadcast_to(add[:, 255:256], (4, 128))],
+
+    turned = pltpu.roll(total, 64, axis=1)
+    q = [total[2 + j:3 + j] for j in range(5)] + [turned[2 + j:3 + j] for j in range(5)]
+    pair = {(0, 0): q[0], (1, 1): q[1], (2, 2): q[2], (1, 0): q[5], (2, 1): q[6], (2, 0): q[8]}
+    x = ldl_solve(lambda i, j: pair[(i, j)], [q[4], q[9], q[7]])
+    x = pltpu.roll(jnp.concatenate(x + [jnp.zeros((5, 128), F32)], axis=0), 64, axis=1)
+    last = jnp.concatenate(
+        [jnp.broadcast_to(add[:, 255:256], (4, 128)), jnp.broadcast_to(mul[:, 255:256], (4, 128))],
         axis=0,
     )
-
-    def carry_copy(i, slot):
-        to = lax.rem(w + i, wide)
+    lane8 = lax.broadcasted_iota(jnp.int32, (8, 128), 1)
+    far_msg = jnp.where(lane8 < 64, last, x)
+    near_msg = jnp.concatenate([add[:, 0:128], add[:, 128:256]], axis=0)
+    mine_buf[0] = near_msg
+    mine_buf[1] = far_msg
+    recv2[me] = near_msg
+
+    def second_copy(i, tw, tn, slot):
+        kind = 0 if isinstance(i, int) else 1
         return pltpu.make_async_remote_copy(
-            src_ref=carry_buf.at[w],
-            dst_ref=carry_buf.at[slot],
-            send_sem=carry_send.at[i],
-            recv_sem=carry_recv.at[slot],
-            device_id=(to, n),
+            src_ref=mine_buf.at[kind],
+            dst_ref=recv2.at[slot],
+            send_sem=send_sem2.at[i],
+            recv_sem=recv_sem2.at[slot],
+            device_id=(tw, tn),
             device_id_type=mesh_id,
         )
 
-    for i in range(1, wide):
-        carry_copy(i, w).start()
-    for i in range(1, SPLIT):
-        cal_copy(i, lax.rem(mine + SPLIT - i, SPLIT)).wait_recv()
+    def second_start(i, tw, tn, c):
+        second_copy(i, tw, tn, me).start()
+        return c
+
+    others(second_start, 0, 1)
+
+    def second_wait(i, tw, tn, c):
+        second_copy(i, tw, tn, tw * narrow + tn).wait_recv()
+        return c
+
+    others(second_wait, 0, -1)
+
+    base = (w // SPLIT) * SPLIT
     for j in range(SPLIT):
-        cal_out[j] = cal_buf[j]
-    for i in range(1, wide):
-        carry_copy(i, lax.rem(w + wide - i, wide)).wait_recv()
+        cal_out[j] = jnp.where(base + j == w, far_msg, recv2[(base + j) * narrow + n])
+    whole = recv2[w * narrow]
+    for k in range(1, narrow):
+        whole = whole + recv2[w * narrow + k]
     state = jnp.zeros((4, 128), F32)
     for p in range(wide):
-        piece = carry_buf[p]
-        state = jnp.where(p < w, piece[0:4] * state + piece[4:8], state)
-    att_out[...] = add + mul * jnp.concatenate([state, state], axis=1)
-
-    def drain(i, c):
-        block_copy(i, me).wait_send()
+        entry = recv2[p * narrow]
+        part, rate = entry[0:4], entry[4:8]
+        for k in range(1, narrow):
+            part = part + recv2[p * narrow + k, 0:4, :]
+        state = jnp.where(p < w, rate * state + part, state)
+    entering = jnp.broadcast_to(state[:, 0:1], (4, 256))
+    att_out[...] = jnp.concatenate([whole[0:4], whole[4:8]], axis=1) + mul * entering
+
+    def drain(i, tw, tn, c):
+        first_copy(i, tw, tn, me).wait_send()
+        second_copy(i, tw, tn, me).wait_send()
         return c
 
-    lax.fori_loop(1, count, drain, 0)
-    for i in range(1, SPLIT):
-        cal_copy(i, mine).wait_send()
-    for i in range(1, wide):
-        carry_copy(i, w).wait_send()
+    others(drain, 0, 1)
 
 
 def on_device(
@@ -352,14 +386,15 @@
     slots = prefit_resid.shape[0]
     count = wide * narrow
     vmem = pl.BlockSpec(memory_space=pltpu.VMEM)
+    hbm = pl.BlockSpec(memory_space=pltpu.HBM)
     row = lambda v: v.reshape(1, slots)
     source_update, send = pl.pallas_call(
         functools.partial(local_kernel, blocks, wide, narrow),
         out_shape=(
             jax.ShapeDtypeStruct((5, blocks * SRC_BLK), F32),
-            jax.ShapeDtypeStruct((count, ROWS, 128), F32),
+            jax.ShapeDtypeStruct((count, 8, 128), F32),
         ),
-        in_specs=[pl.BlockSpec(memory_space=pltpu.SMEM)] + [vmem] * 9,
+        in_specs=[pl.BlockSpec(memory_space=pltpu.SMEM)] + [hbm] * 9,
         out_specs=(vmem, vmem),
         scratch_shapes=[
             pltpu.VMEM((8, slots), F32),
@@ -367,13 +402,23 @@
             pltpu.VMEM((8 * blocks, 128), F32),
             pltpu.VMEM((256, 128), BF16),
             pltpu.VMEM((wide * 32, 256), F32),
-            pltpu.VMEM((narrow * SPLIT // 2 * 32, 256), F32),
+            pltpu.VMEM((narrow * 2 * 32, 256), F32),
+            pltpu.VMEM((1, slots), F32),
+            pltpu.VMEM((5, slots), F32),
+            pltpu.VMEM((1, slots), jnp.int32),
+            pltpu.VMEM((4, slots), F32),
+            pltpu.VMEM((1, slots), F32),
+            pltpu.VMEM((3, slots), F32),
+            pltpu.VMEM((1, slots), jnp.int32),
+            pltpu.VMEM((1, slots), jnp.int32),
+            pltpu.VMEM((1, slots), jnp.int32),
+            pltpu.SemaphoreType.DMA((9,)),
         ],
         compiler_params=pltpu.CompilerParams(vmem_limit_bytes=56 * 1024 * 1024),
         name="local_sums",
     )(
-        block_count, row(prefit_resid), source_partials, attitude_partials, row(spline_position),
-        calib_partials, row(obs_source), row(obs_range), row(obs_knot), row(obs_unit),
+        block_count, row(prefit_resid), source_partials, row(obs_source), attitude_partials,
+        row(spline_position), calib_partials, row(obs_range), row(obs_knot), row(obs_unit),
     )
     dma = pltpu.SemaphoreType.DMA
     attitude_update, cal = pl.pallas_call(
@@ -382,25 +427,23 @@
             jax.ShapeDtypeStruct(knot_decay.shape, F32),
             jax.ShapeDtypeStruct((SPLIT, 8, 128), F32),
         ),
-        in_specs=[vmem, pl.BlockSpec(memory_space=pl.ANY), vmem],
+        in_specs=[hbm, hbm, hbm],
         out_specs=(vmem, vmem),
         scratch_shapes=[
-            pltpu.VMEM((count, ROWS, 128), F32),
-            pltpu.VMEM(given_inverse.shape[1:], F32),
-            pltpu.VMEM((wide, 8, 128), F32),
-            pltpu.VMEM((SPLIT, 8, 128), F32),
-            dma,
-            dma((count,)), dma((count,)),
-            dma((wide,)), dma((wide,)),
-            dma((SPLIT,)), dma((SPLIT,)),
+            pltpu.VMEM((count, 8, 128), F32),
+            pltpu.VMEM((2, 8, 128), F32),
+            pltpu.VMEM((count, 8, 128), F32),
+            pltpu.VMEM((256, 1024), F32),
+            pltpu.VMEM(knot_decay.shape, F32),
+            dma((count,)), dma((count,)), dma((count,)), dma((count,)), dma((3,)),
         ],
         compiler_params=pltpu.CompilerParams(
-            collective_id=0, has_side_effects=True, vmem_limit_bytes=32 * 1024 * 1024
+            collective_id=0, has_side_effects=True, vmem_limit_bytes=56 * 1024 * 1024
         ),
         name="exchange",
     )(send, given_inverse, knot_decay)
     per = CAL // (narrow * SPLIT)
-    cal_update = cal[:, 0:3, 0:per].transpose(1, 0, 2).reshape(3, SPLIT * per)
+    cal_update = cal[:, 0:3, 64:64 + per].transpose(1, 0, 2).reshape(3, SPLIT * per)
     return (source_update, attitude_update, cal_update)
 
 

time: 60.8 us -> 48.7 us (0.80)
  Pallas kernels: 54.7 us -> 45.1 us
  local copies, waits for them, and re-layouts: 5.15 us -> 2.79 us
    pallas_call x1, Pallas kernels: 30.5 us -> 24.4 us  [on_device(): pl.pallas_call(functools.partial(local_kernel, blocks, wide, narrow), out...]
    pallas_call x1, Pallas kernels: 24.2 us -> 20.6 us  [on_device(): pl.pallas_call(functools.partial(exchange_kernel, wide, narrow), out_shap...]
    unnamed x7 -> x1, local copies, waits for them, and re-layouts: 4.46 us -> 1.27 us
    transpose x2, local copies, waits for them, and re-layouts: 0.01 us -> 0.84 us  [on_device(): cal[:, 0:3, 64:64 + per].transpose(1, 0, 2).reshape(3, SPLIT * per)]
where the time goes in v2:
time: 48.7 us; the launch traced here: 48.5 us
  Pallas kernels  45.1 us (93%)
  local copies, waits for them, and re-layouts  2.79 us (6%)
  between operations  0.65 us (1%)
    pallas_call x1, Pallas kernels, on_device(): pl.pallas_call(functools.partial(local_kernel, blocks, wide, narrow), out...  24.4 us
    pallas_call x1, Pallas kernels, on_device(): pl.pallas_call(functools.partial(exchange_kernel, wide, narrow), out_shap...  20.6 us
    unnamed x1, local copies, waits for them, and re-layouts  1.27 us

profile of v2, /device:TPU:0, one launch (start us, length us, event | category | flops | bytes accessed | tf_op | source)
XLA Modules:
  0.0 48.5 jit_solution(15828633802509833969)
XLA Ops:
  0.6 24.4 %local_sums.1 = (f32[5,8192]{1,0:T(8,128)}, f32[32,8,128]{2,1,0:T(8,128)}) custom-call(s32[64]{0:T(128)} %count_ref.1, f32[1,40960]{1,0:T(1,128)} %bitcast.8, f32[5,40960]{1,0:T(8,128)} %sp_hbm.1, s32[1,40960]{1,0:T(1,128)} %bitcast.9, f32[4,40960]{1,0:T(4,128)} %att_hbm.1, f32[1,40960]{1,0:T(1,128)} %bitcast.10, f32[3,40960]{1,0:T(4,128)} %cal_hbm.1, ...), custom_call_target="tpu_custom_call" | custom-call | tf_op jit(solution)/shard_map/local_sums/pallas_call | solution.py:391
  25.1 20.6 %exchange.1 = (f32[4,256]{1,0:T(4,128)}, f32[8,8,128]{2,1,0:T(8,128)}) custom-call(f32[32,8,128]{2,1,0:T(8,128)} %get-tuple-element.8.send_ref, f32[1,1024,1024]{2,1,0:T(8,128)} %inverse_ref.1, f32[4,256]{1,0:T(4,128)} %decay_hbm.1), custom_call_target="tpu_custom_call" | custom-call | tf_op jit(solution)/shard_map/exchange/pallas_call | solution.py:424
  45.7 0.8 %slice_bitcast_fusion = f32[3,8,63]{2,0,1:T(4,128)S(1)} fusion(f32[8,8,128]{2,1,0:T(8,128)} %get-tuple-element.10), kind=kLoop, calls=%fused_computation | loop fusion | bytes 12096 | tf_op jit(solution)/shard_map/transpose | solution.py:446
  46.5 0.7 %reshape.33 = f32[3,504]{1,0:T(4,128)} reshape(f32[3,8,63]{2,1,0:T(8,128)S(1)} %copy.15) | data formatting | bytes 12096 | tf_op jit(solution)/shard_map/reshape | solution.py:446
  47.2 1.3 %copy.17 = f32[4,256]{1,0:T(4,128)} copy(f32[4,256]{1,0:T(4,128)} %get-tuple-element.15) | data formatting | bytes 8192
  (1 shorter events, 0.0 us)

commit v3 on v2

--- a/solution.py
+++ b/solution.py
@@ -98,7 +98,7 @@
         s_ref[pl.ds(b, 40, stride=blocks), :] = sums[0:40] + sums[40:80] + sums[80:120]
         return carry
 
-    lax.fori_loop(0, blocks, normals, 0, unroll=4)
+    lax.fori_loop(0, blocks, normals, 0, unroll=8)
 
     group = 16
     for g in range(0, blocks, group):
@@ -197,7 +197,7 @@
         acc_cal[...] += lax.dot_general(left, hot, NT, preferred_element_type=F32)
         return carry
 
-    lax.fori_loop(0, blocks // 2, rest, 0, unroll=2)
+    lax.fori_loop(0, blocks // 2, rest, 0, unroll=4)
 
     lane = lax.broadcasted_iota(jnp.int32, (4, 256), 1)
     cal_pieces = []
@@ -221,80 +221,84 @@
             total = total + jnp.where(lane >= k, rolled[k], wrapped)
         before = rolled
         for n in range(narrow):
-            d = r * narrow + n
-            send_ref[d, 0:1, :] = total[n:n + 1, 0:128]
-            send_ref[d, 1:2, :] = total[n:n + 1, 128:256]
-            send_ref[d, 2:7, :] = cal_pieces[n * SPLIT + r % SPLIT]
-            send_ref[d, 7:8, :] = jnp.zeros((1, 128), F32)
+            send_ref[n, r, 0:1, :] = total[n:n + 1, 0:128]
+            send_ref[n, r, 1:2, :] = total[n:n + 1, 128:256]
+            send_ref[n, r, 2:7, :] = cal_pieces[n * SPLIT + r % SPLIT]
+            send_ref[n, r, 7:8, :] = jnp.zeros((1, 128), F32)
 
 
 def exchange_kernel(
     wide, narrow,
     send_ref, inverse_ref, decay_hbm,
     att_out, cal_out,
-    recv, mine_buf, recv2, g_ref, decay_ref,
-    send_sem, recv_sem, send_sem2, recv_sem2, local_sem,
+    recv_a, sum_a, recv_b, near_buf, recv_c, far_buf, recv_d, g_ref, decay_ref,
+    send_a, got_a, send_b, got_b, send_c, got_c, send_d, got_d, local_sem,
 ):
     w = lax.axis_index("wide")
     n = lax.axis_index("narrow")
-    me = w * narrow + n
     mesh_id = pl.DeviceIdType.MESH
     own = pl.ds(pl.multiple_of(n * 256, 256), 256)
     loads = [
-        pltpu.make_async_copy(send_ref.at[me], recv.at[me], local_sem.at[0]),
+        pltpu.make_async_copy(send_ref.at[n], recv_a.at[n], local_sem.at[0]),
         pltpu.make_async_copy(inverse_ref.at[0, own], g_ref, local_sem.at[1]),
         pltpu.make_async_copy(decay_hbm, decay_ref, local_sem.at[2]),
     ]
     for load in loads:
         load.start()
 
-    def others(visit, carry, sign):
-        ns = [lax.rem(n + (sign * dn) % narrow, narrow) for dn in range(narrow)]
-        for dn in range(1, narrow):
-            carry = visit(dn, w, ns[dn], carry)
-
-        def row(dw, carry):
-            to = lax.rem(w + wide + sign * dw, wide)
-            for dn in range(narrow):
-                carry = visit(dw * narrow + dn, to, ns[dn], carry)
-            return carry
-
-        return lax.fori_loop(1, wide, row, carry)
-
     barrier = pltpu.get_barrier_semaphore()
-
-    def greet(i, tw, tn, c):
-        pl.semaphore_signal(barrier, inc=1, device_id=(tw, tn), device_id_type=mesh_id)
-        return c
-
-    others(greet, 0, 1)
-    pl.semaphore_wait(barrier, wide * narrow - 1)
-
-    def first_copy(i, tw, tn, slot):
+    narrow_to = [lax.rem(n + i, narrow) for i in range(narrow)]
+    wide_to = [lax.rem(w + i, wide) for i in range(wide)]
+    for i in range(1, narrow):
+        pl.semaphore_signal(barrier, inc=1, device_id=(w, narrow_to[i]), device_id_type=mesh_id)
+    for i in range(1, wide):
+        pl.semaphore_signal(barrier, inc=1, device_id=(wide_to[i], n), device_id_type=mesh_id)
+    pl.semaphore_wait(barrier, narrow + wide - 2)
+
+    def over_narrow(src, dst, send_sem, got_sem, i):
         return pltpu.make_async_remote_copy(
-            src_ref=send_ref.at[tw * narrow + tn],
-            dst_ref=recv.at[slot],
-            send_sem=send_sem.at[i],
-            recv_sem=recv_sem.at[slot],
-            device_id=(tw, tn),
-            device_id_type=mesh_id,
-        )
-
-    def first_start(i, tw, tn, c):
-        first_copy(i, tw, tn, me).start()
-        return c
-
-    others(first_start, 0, 1)
-
-    def collect(i, tw, tn, total):
-        s = tw * narrow + tn
-        first_copy(i, tw, tn, s).wait_recv()
-        return total + recv[s]
-
-    for load in loads:
+            src_ref=src, dst_ref=dst, send_sem=send_sem.at[i], recv_sem=got_sem,
+            device_id=(w, narrow_to[i]), device_id_type=mesh_id,
+        )
+
+    def over_wide(src, dst, send_sem, got_sem, i):
+        return pltpu.make_async_remote_copy(
+            src_ref=src, dst_ref=dst, send_sem=send_sem.at[i], recv_sem=got_sem,
+            device_id=(wide_to[i], n), device_id_type=mesh_id,
+        )
+
+    sends = [
+        over_narrow(send_ref.at[narrow_to[i]], recv_a.at[n], send_a, got_a.at[n], i)
+        for i in range(1, narrow)
+    ]
+    for copy in sends:
+        copy.start()
+    loads[0].wait()
+    for i in range(1, narrow):
+        s = narrow_to[i]
+        over_narrow(send_ref.at[s], recv_a.at[s], send_a, got_a.at[s], i).wait_recv()
+    part = recv_a[0]
+    for k in range(1, narrow):
+        part = part + recv_a[k]
+    sum_a[...] = part
+
+    later = [
+        over_wide(sum_a.at[wide_to[i]], recv_b.at[w], send_b, got_b.at[w], i)
+        for i in range(1, wide)
+    ]
+    for copy in later:
+        copy.start()
+    sends = sends + later
+    recv_b[w] = sum_a[w]
+    for i in range(1, wide):
+        s = wide_to[i]
+        over_wide(sum_a.at[s], recv_b.at[s], send_b, got_b.at[s], i).wait_recv()
+    total = recv_b[0]
+    for k in range(1, wide):
+        total = total + recv_b[k]
+
+    for load in loads[1:]:
         load.wait()
-    total = others(collect, recv[me], -1)
-
     columns = total.T
     y = jnp.zeros((8, 1024), F32)
     for r in range(2):
@@ -312,68 +316,63 @@
         add = add + mul * jnp.where(inside, pltpu.roll(add, step, axis=1), 0.0)
         mul = mul * jnp.where(inside, pltpu.roll(mul, step, axis=1), 1.0)
         step *= 2
+    near_buf[...] = jnp.concatenate([add[:, 0:128], add[:, 128:256]], axis=0)
+    later = [
+        over_narrow(near_buf, recv_c.at[n], send_c, got_c.at[n], i) for i in range(1, narrow)
+    ]
+    for copy in later:
+        copy.start()
+    sends = sends + later
+    recv_c[n] = near_buf[...]
 
     turned = pltpu.roll(total, 64, axis=1)
     q = [total[2 + j:3 + j] for j in range(5)] + [turned[2 + j:3 + j] for j in range(5)]
     pair = {(0, 0): q[0], (1, 1): q[1], (2, 2): q[2], (1, 0): q[5], (2, 1): q[6], (2, 0): q[8]}
     x = ldl_solve(lambda i, j: pair[(i, j)], [q[4], q[9], q[7]])
     x = pltpu.roll(jnp.concatenate(x + [jnp.zeros((5, 128), F32)], axis=0), 64, axis=1)
+
+    for i in range(1, narrow):
+        s = narrow_to[i]
+        over_narrow(near_buf, recv_c.at[s], send_c, got_c.at[s], i).wait_recv()
+    whole = recv_c[0]
+    for k in range(1, narrow):
+        whole = whole + recv_c[k]
+    add = jnp.concatenate([whole[0:4], whole[4:8]], axis=1)
     last = jnp.concatenate(
         [jnp.broadcast_to(add[:, 255:256], (4, 128)), jnp.broadcast_to(mul[:, 255:256], (4, 128))],
         axis=0,
     )
     lane8 = lax.broadcasted_iota(jnp.int32, (8, 128), 1)
-    far_msg = jnp.where(lane8 < 64, last, x)
-    near_msg = jnp.concatenate([add[:, 0:128], add[:, 128:256]], axis=0)
-    mine_buf[0] = near_msg
-    mine_buf[1] = far_msg
-    recv2[me] = near_msg
-
-    def second_copy(i, tw, tn, slot):
-        kind = 0 if isinstance(i, int) else 1
-        return pltpu.make_async_remote_copy(
-            src_ref=mine_buf.at[kind],
-            dst_ref=recv2.at[slot],
-            send_sem=send_sem2.at[i],
-            recv_sem=recv_sem2.at[slot],
-            device_id=(tw, tn),
-            device_id_type=mesh_id,
-        )
-
-    def second_start(i, tw, tn, c):
-        second_copy(i, tw, tn, me).start()
-        return c
-
-    others(second_start, 0, 1)
-
-    def second_wait(i, tw, tn, c):
-        second_copy(i, tw, tn, tw * narrow + tn).wait_recv()
-        return c
-
-    others(second_wait, 0, -1)
+    far_buf[...] = jnp.where(lane8 < 64, last, x)
+    later = [
+        over_wide(far_buf, recv_d.at[w], send_d, got_d.at[w], i) for i in range(1, wide)
+    ]
+    for copy in later:
+        copy.start()
+    sends = sends + later
+    recv_d[w] = far_buf[...]
+    for i in range(1, wide):
+        s = wide_to[i]
+        over_wide(far_buf, recv_d.at[s], send_d, got_d.at[s], i).wait_recv()
 
     base = (w // SPLIT) * SPLIT
     for j in range(SPLIT):
-        cal_out[j] = jnp.where(base + j == w, far_msg, recv2[(base + j) * narrow + n])
-    whole = recv2[w * narrow]
-    for k in range(1, narrow):
-        whole = whole + recv2[w * narrow + k]
+        cal_out[j] = recv_d[base + j]
     state = jnp.zeros((4, 128), F32)
     for p in range(wide):
-        entry = recv2[p * narrow]
-        part, rate = entry[0:4], entry[4:8]
-        for k in range(1, narrow):
-            part = part + recv2[p * narrow + k, 0:4, :]
-        state = jnp.where(p < w, rate * state + part, state)
-    entering = jnp.broadcast_to(state[:, 0:1], (4, 256))
-    att_out[...] = jnp.concatenate([whole[0:4], whole[4:8]], axis=1) + mul * entering
-
-    def drain(i, tw, tn, c):
-        first_copy(i, tw, tn, me).wait_send()
-        second_copy(i, tw, tn, me).wait_send()
-        return c
-
-    others(drain, 0, 1)
+        entry = recv_d[p]
+        state = jnp.where(p < w, entry[4:8] * state + entry[0:4], state)
+    att_out[...] = add + mul * jnp.broadcast_to(state[:, 0:1], (4, 256))
+    for copy in sends:
+        copy.wait_send()
+
+
+def finish_kernel(att_ref, cal_ref, att_out, cal_out):
+    att_out[...] = att_ref[...]
+    per = cal_out.shape[1] // SPLIT
+    cal_out[...] = jnp.concatenate(
+        [cal_ref[j, 0:3, 64:64 + per] for j in range(SPLIT)], axis=1
+    )
 
 
 def on_device(
@@ -384,7 +383,6 @@
     narrow = lax.axis_size("narrow")
     blocks = block_count.shape[0]
     slots = prefit_resid.shape[0]
-    count = wide * narrow
     vmem = pl.BlockSpec(memory_space=pltpu.VMEM)
     hbm = pl.BlockSpec(memory_space=pltpu.HBM)
     row = lambda v: v.reshape(1, slots)
@@ -392,7 +390,7 @@
         functools.partial(local_kernel, blocks, wide, narrow),
         out_shape=(
             jax.ShapeDtypeStruct((5, blocks * SRC_BLK), F32),
-            jax.ShapeDtypeStruct((count, 8, 128), F32),
+            jax.ShapeDtypeStruct((narrow, wide, 8, 128), F32),
         ),
         in_specs=[pl.BlockSpec(memory_space=pltpu.SMEM)] + [hbm] * 9,
         out_specs=(vmem, vmem),
@@ -421,7 +419,7 @@
         row(spline_position), calib_partials, row(obs_range), row(obs_knot), row(obs_unit),
     )
     dma = pltpu.SemaphoreType.DMA
-    attitude_update, cal = pl.pallas_call(
+    attitude_raw, cal = pl.pallas_call(
         functools.partial(exchange_kernel, wide, narrow),
         out_shape=(
             jax.ShapeDtypeStruct(knot_decay.shape, F32),
@@ -430,20 +428,35 @@
         in_specs=[hbm, hbm, hbm],
         out_specs=(vmem, vmem),
         scratch_shapes=[
-            pltpu.VMEM((count, 8, 128), F32),
-            pltpu.VMEM((2, 8, 128), F32),
-            pltpu.VMEM((count, 8, 128), F32),
+            pltpu.VMEM((narrow, wide, 8, 128), F32),
+            pltpu.VMEM((wide, 8, 128), F32),
+            pltpu.VMEM((wide, 8, 128), F32),
+            pltpu.VMEM((8, 128), F32),
+            pltpu.VMEM((narrow, 8, 128), F32),
+            pltpu.VMEM((8, 128), F32),
+            pltpu.VMEM((wide, 8, 128), F32),
             pltpu.VMEM((256, 1024), F32),
             pltpu.VMEM(knot_decay.shape, F32),
-            dma((count,)), dma((count,)), dma((count,)), dma((count,)), dma((3,)),
+            dma((narrow,)), dma((narrow,)), dma((wide,)), dma((wide,)),
+            dma((narrow,)), dma((narrow,)), dma((wide,)), dma((wide,)),
+            dma((3,)),
         ],
         compiler_params=pltpu.CompilerParams(
             collective_id=0, has_side_effects=True, vmem_limit_bytes=56 * 1024 * 1024
         ),
         name="exchange",
     )(send, given_inverse, knot_decay)
-    per = CAL // (narrow * SPLIT)
-    cal_update = cal[:, 0:3, 64:64 + per].transpose(1, 0, 2).reshape(3, SPLIT * per)
+    attitude_update, cal_update = pl.pallas_call(
+        finish_kernel,
+        out_shape=(
+            jax.ShapeDtypeStruct(knot_decay.shape, F32),
+            jax.ShapeDtypeStruct((3, CAL // narrow), F32),
+        ),
+        in_specs=[vmem, vmem],
+        out_specs=(vmem, vmem),
+        compiler_params=pltpu.CompilerParams(vmem_limit_bytes=56 * 1024 * 1024),
+        name="finish",
+    )(attitude_raw, cal)
     return (source_update, attitude_update, cal_update)
 
 

time: 48.7 us -> 45.4 us (0.932)
  local copies, waits for them, and re-layouts: 2.79 us -> 0 us
  Pallas kernels: 45.1 us -> 44.6 us
    pallas_call x1, Pallas kernels: 24.4 us -> 21.2 us  [on_device(): pl.pallas_call(functools.partial(local_kernel, blocks, wide, narrow), out...]
    pallas_call x0 -> x1, Pallas kernels: none -> 1.44 us  [on_device(): pl.pallas_call(finish_kernel, out_shape=(jax.ShapeDtypeStruct(knot_decay....]
    pallas_call x1, Pallas kernels: 20.6 us -> 21.9 us  [on_device(): pl.pallas_call(functools.partial(exchange_kernel, wide, narrow), out_shap...]
    unnamed x1 -> x0, local copies, waits for them, and re-layouts: 1.27 us -> none
    transpose x2 -> x0, local copies, waits for them, and re-layouts: 0.84 us -> none  [on_device(): cal[:, 0:3, 64:64 + per].transpose(1, 0, 2).reshape(3, SPLIT * per)]
    reshape x1 -> x0, local copies, waits for them, and re-layouts: 0.69 us -> none  [on_device(): cal[:, 0:3, 64:64 + per].transpose(1, 0, 2).reshape(3, SPLIT * per)]
where the time goes in v3:
time: 45.4 us; the launch traced here: 45.2 us
  Pallas kernels  44.6 us (98%)
  between operations  0.65 us (1%)
    pallas_call x1, Pallas kernels, on_device(): pl.pallas_call(functools.partial(exchange_kernel, wide, narrow), out_shap...  21.9 us
    pallas_call x1, Pallas kernels, on_device(): pl.pallas_call(functools.partial(local_kernel, blocks, wide, narrow), out...  21.2 us
    pallas_call x1, Pallas kernels, on_device(): pl.pallas_call(finish_kernel, out_shape=(jax.ShapeDtypeStruct(knot_decay....  1.44 us

profile of v3, /device:TPU:0, one launch (start us, length us, event | category | flops | bytes accessed | tf_op | source)
XLA Modules:
  0.0 45.2 jit_solution(15469730590756901041)
XLA Ops:
  0.6 21.2 %local_sums.1 = (f32[5,8192]{1,0:T(8,128)}, f32[4,8,8,128]{3,2,1,0:T(8,128)}) custom-call(s32[64]{0:T(128)} %count_ref.1, f32[1,40960]{1,0:T(1,128)} %bitcast.6, f32[5,40960]{1,0:T(8,128)} %sp_hbm.1, s32[1,40960]{1,0:T(1,128)} %bitcast.7, f32[4,40960]{1,0:T(4,128)} %att_hbm.1, f32[1,40960]{1,0:T(1,128)} %bitcast.8, f32[3,40960]{1,0:T(4,128)} %cal_hbm.1, ...), custom_call_target="tpu_custom_call" | custom-call | tf_op jit(solution)/shard_map/local_sums/pallas_call | solution.py:389
  21.9 21.9 %exchange.1 = (f32[4,256]{1,0:T(4,128)}, f32[8,8,128]{2,1,0:T(8,128)}) custom-call(f32[4,8,8,128]{3,2,1,0:T(8,128)} %get-tuple-element.10.send_ref, f32[1,1024,1024]{2,1,0:T(8,128)} %inverse_ref.1, f32[4,256]{1,0:T(4,128)} %decay_hbm.1), custom_call_target="tpu_custom_call" | custom-call | tf_op jit(solution)/shard_map/exchange/pallas_call | solution.py:422
  43.8 1.4 %finish.1 = (f32[4,256]{1,0:T(4,128)}, f32[3,504]{1,0:T(4,128)}) custom-call(f32[4,256]{1,0:T(4,128)} %get-tuple-element.11.att_ref, f32[8,8,128]{2,1,0:T(8,128)} %get-tuple-element.12.cal_ref), custom_call_target="tpu_custom_call" | custom-call | tf_op jit(solution)/shard_map/finish/pallas_call | solution.py:449
